TPU v7x, 32 devices: a whole 2x2x4 slice. The times are simulated.
32 devices in a mesh: ctx: 8 (over z, x), own: 4 (over y, core).
Axes of the slice: x: 2, y: 2, z: 4, core: 2. Of those that a mesh axis runs over, the one named last changes fastest.
Arguments:
- query_proj: bfloat16 [4096, 8192], P(('ctx', 'own')), may hold values from -6 to 6
- key_proj: bfloat16 [4096, 8192], P(('ctx', 'own')), may hold values from -6 to 6
- value_proj: bfloat16 [4096, 8192], P(('ctx', 'own')), may hold values from -6 to 6
- short_taps: float32 [3, 7, 512], P(None, None, 'own'), may hold values from -2 to 2
- long_taps: float32 [128, 512], P(None, 'own'), may hold values from -0.5 to 0.5
- decay_rate: float32 [8, 8192], P(None, 'own'), may hold values from 1.2207031e-05 to 0.03
- residues: float32 [8, 8192], P(None, 'own'), may hold values from -2 to 2
- grad_out: bfloat16 [4096, 8192], P(('ctx', 'own')), may hold values from -6 to 6
Outputs:
- layer_out: bfloat16 [4096, 8192], P(('ctx', 'own'))
- grad_query: bfloat16 [4096, 8192], P(('ctx', 'own'))
- grad_key: bfloat16 [4096, 8192], P(('ctx', 'own'))
- grad_value: bfloat16 [4096, 8192], P(('ctx', 'own'))
- grad_long_taps: float32 [128, 512], P(None, 'own')
All inputs are finite; a program needn't handle non-finite values.
Results may differ from a plain program's by a relative error of at most 0.02.
Values may be sent and summed in bfloat16 or wider, within the bound.
A program may use at most 256 MiB of HBM per device.

v0:
```python
import math

import jax
import jax.numpy as jnp
from jax import lax
from jax.sharding import PartitionSpec as P

CPG = 16


exact_mode = lax.Precision.HIGHEST


def from_behind(value, axis, steps):
    count = lax.axis_size(axis)
    leading, last = (max(0, -steps), min(count, count - steps))
    return lax.ppermute(value, axis, [(source, source + steps) for source in range(leading, last)])


def carried_in(x, axis, combine, identity, reverse):
    size, index = (lax.axis_size(axis), lax.axis_index(axis))
    everything = jax.tree.map(
        lambda part, kind: lax.all_gather(part.astype(kind), axis), x, (jnp.bfloat16, jnp.bfloat16)
    )
    start = jax.tree.map(
        lambda part, zero: jnp.broadcast_to(jnp.asarray(zero, part.dtype), part.shape), x, identity
    )

    def hop(k, before):
        at = size - 1 - k if reverse else k
        reached = at > index if reverse else at < index
        new = combine(
            before, jax.tree.map(lambda part, own: part[at].astype(own.dtype), everything, x)
        )
        return jax.tree.map(lambda a, b: jnp.where(reached, a, b), new, before)

    return lax.fori_loop(0, size, hop, start)


def tables(row_count):
    bin_count = row_count + 1
    freq_index = jnp.arange(bin_count, dtype=jnp.int32)[:, None]
    place_index = jnp.arange(row_count, dtype=jnp.int32)[None, :]
    phase_index = freq_index * place_index % (2 * row_count)
    angle_all = phase_index.astype(jnp.float32) * (math.pi / row_count)
    cos_fwd = jnp.cos(angle_all)
    sin_fwd = jnp.sin(angle_all)
    at_edge = jnp.logical_or(freq_index == 0, freq_index == row_count)
    weight_bin = jnp.where(at_edge, 1.0, 2.0).astype(jnp.float32) / (2.0 * row_count)
    cos_inv = jnp.transpose(cos_fwd * weight_bin)
    sin_inv = jnp.transpose(sin_fwd * weight_bin)
    parity = (1 - 2 * (freq_index % 2)).astype(jnp.float32)
    return (cos_fwd, sin_fwd, cos_inv, sin_inv, parity)


def transform(table_set, rows_in):
    values = rows_in.astype(jnp.float32)
    real_part = jnp.dot(
        table_set[0], values, precision=exact_mode, preferred_element_type=jnp.float32
    )
    imag_part = -jnp.dot(
        table_set[1], values, precision=exact_mode, preferred_element_type=jnp.float32
    )
    return (real_part, imag_part)


def restore(table_set, real_part, imag_part):
    first = jnp.dot(
        table_set[2], real_part, precision=exact_mode, preferred_element_type=jnp.float32
    )
    return first - jnp.dot(
        table_set[3], imag_part, precision=exact_mode, preferred_element_type=jnp.float32
    )


def featurize(rim_part, main_rows, taps_chan):
    joined = jnp.concatenate([rim_part, main_rows], axis=0).astype(jnp.float32)
    row_count = main_rows.shape[0]
    tap_count = taps_chan.shape[0]
    summed = jnp.zeros(main_rows.shape, jnp.float32)
    for offset in range(tap_count):
        first_row = tap_count - 1 - offset
        summed = summed + taps_chan[offset][None, :] * joined[first_row : first_row + row_count]
    return summed.astype(jnp.bfloat16)


def unfeaturize(main_rows, rim_part, taps_chan):
    joined = jnp.concatenate([main_rows, rim_part], axis=0).astype(jnp.float32)
    row_count = main_rows.shape[0]
    tap_count = taps_chan.shape[0]
    summed = jnp.zeros(main_rows.shape, jnp.float32)
    for offset in range(tap_count):
        summed = summed + taps_chan[offset][None, :] * joined[offset : offset + row_count]
    return summed.astype(jnp.bfloat16)


def spread(spectrum):
    bin_count, group_count = spectrum.shape
    return jnp.broadcast_to(spectrum[:, :, None], (bin_count, group_count, CPG)).reshape(
        bin_count, group_count * CPG
    )


def modal_weight(decay, resid):
    return resid * jnp.sqrt(-jnp.expm1(-2.0 * decay))


def pole_rows(coeff, decay, lag_rows, scaling):
    summed = jnp.zeros((lag_rows.shape[0], decay.shape[1]), jnp.float32)
    for pole in range(decay.shape[0]):
        summed = summed + (coeff[pole] * scaling[pole])[None, :] * jnp.exp(
            -decay[pole][None, :] * lag_rows[:, None]
        )
    return summed


def pole_states(decay, lag_rows, field):
    states = []
    for pole in range(decay.shape[0]):
        states.append(jnp.sum(jnp.exp(-decay[pole][None, :] * lag_rows[:, None]) * field, axis=0))
    return jnp.stack(states)


def shards(query_proj, key_proj, value_proj, short_taps, long_taps, decay_rate, residues, grad_out):
    row_count, chan_count = query_proj.shape
    rim_rows = short_taps.shape[1] - 1
    table_set = tables(row_count)
    parity = table_set[4]
    lag_index = jnp.arange(row_count, dtype=jnp.float32)
    weight = modal_weight(decay_rate, residues)
    head_rows = pole_rows(weight, decay_rate, lag_index, jnp.ones_like(weight))
    head_re, head_im = transform(table_set, head_rows)
    taps_re, taps_im = transform(table_set, long_taps)
    head_all, taps_all, decay_all, resid_all, short_all = (
        lax.all_gather(jnp.stack([head_re, head_im]), "own", axis=2, tiled=True),
        lax.all_gather(jnp.stack([taps_re, taps_im]), "own", axis=2, tiled=True),
        lax.all_gather(decay_rate, "own", axis=1, tiled=True),
        lax.all_gather(residues, "own", axis=1, tiled=True),
        lax.all_gather(short_taps, "own", axis=2, tiled=True),
    )
    head_re, head_im = (head_all[0], head_all[1])
    edge_re, edge_im = (spread(taps_all[0]), spread(taps_all[1]))
    tap_count = short_all.shape[1]
    group_count = short_all.shape[2]
    short_chan = jnp.broadcast_to(
        short_all[:, :, :, None], (3, tap_count, group_count, CPG)
    ).reshape(3, tap_count, group_count * CPG)
    weight_all = modal_weight(decay_all, resid_all)
    block_rate = decay_all * row_count

    def chain_pair(earlier_pair, later_pair):
        return (
            earlier_pair[0] + later_pair[0],
            jnp.exp(-block_rate * later_pair[0]) * earlier_pair[1] + later_pair[1],
        )

    identity = (jnp.zeros((), jnp.float32), jnp.zeros_like(block_rate))
    one_block = jnp.ones((), jnp.float32)
    rim_set = from_behind(
        (
            query_proj[row_count - rim_rows :],
            key_proj[row_count - rim_rows :],
            value_proj[row_count - rim_rows :],
        ),
        ("ctx", "own"),
        1,
    )
    query_feat = featurize(rim_set[0], query_proj, short_chan[0])
    key_feat = featurize(rim_set[1], key_proj, short_chan[1])
    value_feat = featurize(rim_set[2], value_proj, short_chan[2])
    product = (key_feat.astype(jnp.float32) * value_feat.astype(jnp.float32)).astype(jnp.bfloat16)
    earlier = from_behind(product, ("ctx", "own"), 1)
    product_float = product.astype(jnp.float32)
    block_state = pole_states(decay_all, row_count - 1 - lag_index, product_float)
    state_in = carried_in((one_block, block_state), ("ctx", "own"), chain_pair, identity, False)[1]
    prev_re, prev_im = transform(table_set, earlier)
    own_re, own_im = transform(table_set, product)
    own_re = parity * own_re
    own_im = parity * own_im
    win_re = prev_re + own_re
    win_im = prev_im + own_im
    out_re = win_re * edge_re - win_im * edge_im + own_re * head_re - own_im * head_im
    out_im = win_re * edge_im + win_im * edge_re + own_re * head_im + own_im * head_re
    near_part = restore(table_set, parity * out_re, parity * out_im)
    far_part = pole_rows(weight_all, decay_all, lag_index + 1.0, state_in)
    long_conv = near_part + far_part
    layer_out = (query_feat.astype(jnp.float32) * long_conv).astype(jnp.bfloat16)
    grad_float = grad_out.astype(jnp.float32)
    grad_conv = (grad_float * query_feat.astype(jnp.float32)).astype(jnp.bfloat16)
    grad_qfeat = (grad_float * long_conv).astype(jnp.bfloat16)
    next_grad = from_behind(grad_conv, ("ctx", "own"), -1)
    conv_float = grad_conv.astype(jnp.float32)
    back_state = pole_states(decay_all, lag_index, conv_float)
    state_after = carried_in((one_block, back_state), ("ctx", "own"), chain_pair, identity, True)[1]
    cur_re, cur_im = transform(table_set, grad_conv)
    nxt_re, nxt_im = transform(table_set, next_grad)
    gwin_re = cur_re + parity * nxt_re
    gwin_im = cur_im + parity * nxt_im
    back_re = gwin_re * edge_re + gwin_im * edge_im + cur_re * head_re + cur_im * head_im
    back_im = gwin_im * edge_re - gwin_re * edge_im + cur_im * head_re - cur_re * head_im
    near_back = restore(table_set, back_re, back_im)
    far_back = pole_rows(weight_all, decay_all, row_count - lag_index, state_after)
    grad_prod = near_back + far_back
    grad_kfeat = (grad_prod * value_feat.astype(jnp.float32)).astype(jnp.bfloat16)
    grad_vfeat = (grad_prod * key_feat.astype(jnp.float32)).astype(jnp.bfloat16)
    back_rims = from_behind(
        (grad_qfeat[:rim_rows], grad_kfeat[:rim_rows], grad_vfeat[:rim_rows]), ("ctx", "own"), -1
    )
    grad_query = unfeaturize(grad_qfeat, back_rims[0], short_chan[0])
    grad_key = unfeaturize(grad_kfeat, back_rims[1], short_chan[1])
    grad_value = unfeaturize(grad_vfeat, back_rims[2], short_chan[2])
    corr_re = parity * (cur_re * win_re + cur_im * win_im)
    corr_im = parity * (cur_im * win_re - cur_re * win_im)
    bin_count = corr_re.shape[0]
    all_groups = chan_count // CPG
    corr_re = corr_re.reshape(bin_count, all_groups, CPG).sum(axis=2)
    corr_im = corr_im.reshape(bin_count, all_groups, CPG).sum(axis=2)
    seq_total = row_count * lax.axis_size("ctx") * lax.axis_size("own")
    scale_taps = 1.0 / math.sqrt(seq_total * CPG)
    partial_taps = (
        jnp.dot(table_set[2], corr_re, precision=exact_mode, preferred_element_type=jnp.float32)
        - jnp.dot(table_set[3], corr_im, precision=exact_mode, preferred_element_type=jnp.float32)
    ) * scale_taps
    owned_part = lax.psum_scatter(
        partial_taps.astype(jnp.bfloat16), "own", scatter_dimension=1, tiled=True
    )
    grad_taps = lax.psum(owned_part, "ctx").astype(jnp.float32)
    return (layer_out, grad_query, grad_key, grad_value, grad_taps)


def solution(mesh):
    placed = (
        P(("ctx", "own"), None),
        P(("ctx", "own"), None),
        P(("ctx", "own"), None),
        P(None, None, "own"),
        P(None, "own"),
        P(None, "own"),
        P(None, "own"),
        P(("ctx", "own"), None),
    )
    return jax.shard_map(
        shards,
        mesh=mesh,
        in_specs=placed,
        out_specs=(
            P(("ctx", "own"), None),
            P(("ctx", "own"), None),
            P(("ctx", "own"), None),
            P(("ctx", "own"), None),
            P(None, "own"),
        ),
        check_vma=False,
    )
```

profile of v0, /device:TPU:1, one launch (start us, length us, event | category | flops | bytes accessed | tf_op | source)
XLA Modules:
  0.0 600.4 jit_solution(14067084637219126109)
XLA Ops:
  9.7 4.5 collective-permute-start
  22.7 5.2 all_gather.27
  28.0 6.1 %all_gather.31 = f32[8,8192]{1,0:T(8,128)S(1)} all-gather(f32[8,2048]{1,0:T(8,128)} %param.17), channel_id=1, replica_groups=mesh['ctx'=8,'own'=4] {'own'}, dimensions={1}, use_global_device_ids=true | all-gather | bytes 327680 | tf_op jit(solution)/shard_map/all_gather | solution.py:137
  46.2 24.6 %fusion.62 = (bf16[8192]{0:T(1024)(128)(2,1)}, bf16[8192]{0:T(1024)(128)(2,1)}, bf16[8192]{0:T(1024)(128)(2,1)}, bf16[8192]{0:T(1024)(128)(2,1)}, bf16[8192]{0:T...) fusion(f32[8192]{0:T(1024)S(1)} %bitcast.149, ...), kind=kLoop, calls=%fused_computation.101 | loop fusion | flops 104726528 | bytes 101876224 | tf_op jit(solution)/shard_map/reduce_sum | solution.py:120
  80.2 16.0 %collective-permute-done.3 = bf16[128,8192]{1,0:T(8,128)(2,1)S(1)} collective-permute-done((bf16[128,8192]{1,0:T(8,128)(2,1)S(1)}, bf16[128,8192]{1,0:T(8,128)(2,1)S(1)}, u32[]{:S(2)}, u32[]{:S(2)}) %collective-permute-start.3) | collective-permute-done | bytes 2097184 | tf_op jit(solution)/shard_map/ppermute | solution.py:17
  101.0 7.0 %subtract_multiply_fusion = (f32[129,8192]{1,0:T(8,128)}, f32[129,8192]{1,0:T(8,128)}, f32[129,8192]{1,0:T(8,128)}) fusion(f32[129,8192]{1,0:T(8,128)S(1)} %fusion.6, f32[129,8192]{1,0:T(8,128)S(1)} %convolution_negate_fusion.1, f32[129,8192]{1,0:T(8,128)S(1)} %convolution_add_fusion, f32[129]{0:T(256)S(1)} %fusion.154, ...), kind=kOutput, calls=%fused_computation.46 | convolution fusion | flops 1631880960 | bytes 27460100 | tf_op jit(solution)/shard_map/dot_general | solution.py:58
  108.0 7.5 %copy.35 = f32[129,8192]{0,1:T(8,128)} copy(f32[129,8192]{1,0:T(8,128)} %get-tuple-element.408) | data formatting | bytes 8454144 | tf_op jit(solution)/shard_map/mul | solution.py:212
  115.5 5.2 bitcast_reduce_fusion.1
  120.7 7.5 %copy.36 = f32[129,8192]{0,1:T(8,128)} copy(f32[129,8192]{1,0:T(8,128)} %get-tuple-element.407) | data formatting | bytes 8454144 | tf_op jit(solution)/shard_map/mul | solution.py:213
  128.3 5.2 bitcast_reduce_fusion
  158.5 8.6 %all_gather.28 = f32[2,129,512]{2,1,0:T(8,128)S(1)} all-gather(f32[2,129,128]{2,1,0:T(8,128)S(1)} %pad_maximum_fusion.1), channel_id=1, replica_groups=mesh['ctx'=8,'own'=4] {'own'}, dimensions={2}, use_global_device_ids=true | all-gather | bytes 660480 | tf_op jit(solution)/shard_map/all_gather | solution.py:136
  169.9 5.0 broadcast_in_dim.218
  175.0 8.1 %copy.28 = f32[129,8192]{1,0:T(8,128)} copy(f32[129,8192]{0,1:T(8,128)} %bitcast.143) | data formatting | bytes 8454144 | tf_op jit(solution)/shard_map/reshape | solution.py:99
  185.0 5.0 broadcast_in_dim.216
  190.0 7.7 %copy.26 = f32[129,8192]{1,0:T(8,128)} copy(f32[129,8192]{0,1:T(8,128)} %bitcast.144) | data formatting | bytes 8454144 | tf_op jit(solution)/shard_map/reshape | solution.py:99
  197.8 42.1 %all-reduce = bf16[32]{0:T(256)(128)(2,1)S(1)} all-reduce(bf16[32]{0:T(256)(128)(2,1)S(1)} %dynamic-update-slice), channel_id=1, replica_groups=mesh['ctx'=8,'own'=4] {'ctx','own'}, use_global_device_ids=true, to_apply=%add | all-reduce | flops 32 | bytes 128
  242.9 35.7 %all_gather.30 = f32[8,8192]{1,0:T(8,128)S(1)} all-gather(f32[8,2048]{1,0:T(8,128)S(1)} %copy-done.50), channel_id=1, replica_groups=mesh['ctx'=8,'own'=4] {'own'}, dimensions={1}, use_global_device_ids=true | all-gather | bytes 327680 | tf_op jit(solution)/shard_map/all_gather | solution.py:138
  278.8 6.8 %fusion.3 = f32[129,8192]{1,0:T(8,128)} fusion(f32[129,8192]{1,0:T(8,128)} %copy-done.2, bf16[128,8192]{1,0:T(8,128)(2,1)S(1)} %collective-permute-done.5, f32[129]{0:T(256)S(1)} %copy-done.68), kind=kOutput, calls=%fused_computation.22 | convolution fusion | flops 1626597120 | bytes 10551812 | tf_op jit(solution)/shard_map/dot_general | solution.py:61
  285.7 4.6 fusion.4
  291.2 28.4 %psum.7 = bf16[128,128]{1,0:T(8,128)(2,1)S(1)} all-reduce(bf16[128,128]{1,0:T(8,128)(2,1)S(1)} %copy.38), channel_id=1, replica_groups=mesh['ctx'=8,'own'=4] {'ctx'}, use_global_device_ids=true, to_apply=%region_23.24 | all-reduce | flops 16384 | bytes 65536 | tf_op jit(solution)/shard_map/psum | solution.py:227
  320.2 80.2 %while.33 = (s32[]{:T(128)}, f32[8,8192]{1,0:T(8,128)S(1)}, s32[]{:T(128)}, bf16[32]{0:T(256)(128)(2,1)S(1)}, f32[8,8192]{1,0:T(8,128)S(1)}, /*index=5*/bf16[32,...) while((s32[]{:T(128)}, f32[8,8192]{1,0:T(8,128)S(1)}, s32[]{:T(128)}, ...), condition=%wide.region_19.20_spmd.clone, body=%wide.region_18.19_spmd.clone.sunk | while | flops 393225 | bytes 917701 | solution.py:37
  400.5 76.8 %while.32 = (s32[]{:T(128)}, f32[8,8192]{1,0:T(8,128)S(1)}, s32[]{:T(128)}, bf16[32]{0:T(256)(128)(2,1)S(1)}, f32[8,8192]{1,0:T(8,128)S(1)}, /*index=5*/bf16[32,8,8192]{2,1,0:T(8,128)(2,1)}, s32[]{:T(128)}, s32[]{:T(128)}) while((s32[]{:T(128)}, f32[8,8192]{1,0:T(8,128)S(1)}, s32[]{:T(128)}, bf16[32]{0:T(256)(128)(2,1)S(1)}, ...), condition=%wide.region_9.10_spmd.clone, body=%wide.region_8.9_spmd.clone.sunk | while | flops 393221 | bytes 917639 | solution.py:37
  478.1 18.6 %fusion.32 = f32[128,8192]{1,0:T(8,128)} fusion(f32[129,8192]{1,0:T(8,128)} %copy-done.3, f32[129,8192]{1,0:T(8,128)} %copy-done.4, f32[129,8192]{1,0:T(8,128)} %copy-done.5, f32[129,8192]{1,0:T(8,128)} %copy.28, f32[129,8192]{1,0:T(8,128)} %copy-done.6, f32[129,8192]{1,0:T(8,128)} %copy.26, f32[2,129,8192]{2,1,0:T(8,128)} %all-gather.4.cloned.1.call-done, ...), kind=kOutput, calls=%fused_computation.71 | convolution fusion | flops 1631897472 | bytes 38011912 | tf_op jit(solution)/shard_map/dot_general | solution.py:68
  496.8 20.1 %fusion.8 = f32[128,8192]{1,0:T(8,128)} fusion(f32[128,8192]{1,0:T(8,128)} %fusion.32, f32[129,8192]{1,0:T(8,128)} %copy-done.3, f32[129,8192]{1,0:T(8,128)} %copy-done.4, f32[129,8192]{1,0:T(8,128)} %copy-done.5, f32[129,8192]{1,0:T(8,128)} %copy.26, f32[129,8192]{1,0:T(8,128)} %copy-done.6, f32[129,8192]{1,0:T(8,128)} %copy.28, ...), kind=kOutput, calls=%fused_computation.35 | convolution fusion | flops 1658111872 | bytes 42731016 | tf_op jit(solution)/shard_map/dot_general | solution.py:71
  516.9 5.6 fusion.45
  522.5 9.3 %collective-permute-start.4 = (bf16[6,8192]{1,0:T(8,128)(2,1)S(1)}, bf16[6,8192]{1,0:T(8,128)(2,1)S(1)}, u32[]{:S(2)}, u32[]{:S(2)}) collective-permute-start(bf16[6,8192]{1,0:T(8,128)(2,1)S(1)} %slice.766), channel_id=1, source_target_pairs={{1,0},{2,1},{3,2},{4,3},{5,4},{6,5},{7,6},{8,7},{9,8},{10,9},{11,1... | collective-permute-start | bytes 294920 | tf_op jit(solution)/shard_map/ppermute | solution.py:17
  531.9 17.3 %fusion.16 = f32[128,8192]{1,0:T(8,128)} fusion(f32[129,8192]{1,0:T(8,128)S(1)} %bitcast.140, f32[129,8192]{1,0:T(8,128)} %get-tuple-element.478, f32[129,8192]{1,0:T(8,128)} %fusion.3, f32[129,8192]{1,0:T(8,128)} %copy.28, f32[129,8192]{1,0:T(8,128)} %fusion.4, f32[129,8192]{1,0:T(8,128)} %copy.26, f32[2,129,8192]{2,1,0:T(8,128)} %all-gather.4.cloned.1.call-done, ...), kind=kOutput, calls=%fused_computation.55 | convolution fusion | flops 1630840704 | bytes 38011396 | tf_op jit(solution)/shard_map/dot_general | solution.py:68
  549.2 19.0 %fusion.7 = f32[128,8192]{1,0:T(8,128)} fusion(f32[128,8192]{1,0:T(8,128)} %fusion.16, f32[129,8192]{1,0:T(8,128)} %get-tuple-element.478, f32[129,8192]{1,0:T(8,128)S(1)} %bitcast.140, f32[129,8192]{1,0:T(8,128)} %fusion.4, f32[129,8192]{1,0:T(8,128)} %copy.28, f32[129,8192]{1,0:T(8,128)} %fusion.3, f32[129,8192]{1,0:T(8,128)} %copy.26, ...), kind=kOutput, calls=%fused_computation.33 | convolution fusion | flops 1657055104 | bytes 42730500 | tf_op jit(solution)/shard_map/dot_general | solution.py:71
  568.2 4.5 fusion.42
  577.3 4.7 fusion.78
  582.8 4.4 fusion.71
  588.1 4.4 fusion.64
  (414 shorter events, 189.5 us)
Async XLA Ops:
  8.0 149.4 %copy-start = (f32[128,128]{1,0:T(8,128)S(1)}, f32[128,128]{1,0:T(8,128)}, u32[]{:S(2)}) copy-start(f32[128,128]{1,0:T(8,128)} %param.16) | copy-start | bytes 196612
  8.0 282.3 %reduce-scatter.4.cloned.1.call-start = ((), (), s32[]{:S(2)}) async-start(), calls=%async_computation.4 | async-start | bytes 163840
  9.7 31.2 %collective-permute-start = (bf16[6,8192]{1,0:T(8,128)(2,1)}, bf16[6,8192]{1,0:T(8,128)(2,1)}, u32[]{:S(2)}, u32[]{:S(2)}) collective-permute-start(bf16[6,8192]{1,0:T(8,128)(2,1)} %slice.556), channel_id=1, source_target_pairs={{0,1},{1,2},{2,3},{3,4},{4,5},{5,6},{6,7},{7,8},{8,9},{9,10},{10,1... | collective-permute-start | bytes 294920 | tf_op jit(solution)/shard_map/ppermute | solution.py:17
  15.8 26.7 %collective-permute-start.1 = (bf16[6,8192]{1,0:T(8,128)(2,1)}, bf16[6,8192]{1,0:T(8,128)(2,1)}, u32[]{:S(2)}, u32[]{:S(2)}) collective-permute-start(bf16[6,8192]{1,0:T(8,128)(2,1)} %slice.578), channel_id=1, source_target_pairs={{0,1},{1,2},{2,3},{3,4},{4,5},{5,6},{6,7},{7,8},{8,9},{9,10},{10,1... | collective-permute-start | bytes 294920 | tf_op jit(solution)/shard_map/ppermute | solution.py:17
  19.3 24.9 %collective-permute-start.2 = (bf16[6,8192]{1,0:T(8,128)(2,1)}, bf16[6,8192]{1,0:T(8,128)(2,1)}, u32[]{:S(2)}, u32[]{:S(2)}) collective-permute-start(bf16[6,8192]{1,0:T(8,128)(2,1)} %slice.600), channel_id=1, source_target_pairs={{0,1},{1,2},{2,3},{3,4},{4,5},{5,6},{6,7},{7,8},{8,9},{9,10},{10,1... | collective-permute-start | bytes 294920 | tf_op jit(solution)/shard_map/ppermute | solution.py:17
  70.8 25.3 %collective-permute-start.3 = (bf16[128,8192]{1,0:T(8,128)(2,1)S(1)}, bf16[128,8192]{1,0:T(8,128)(2,1)S(1)}, u32[]{:S(2)}, u32[]{:S(2)}) collective-permute-start(bf16[128,8192]{1,0:T(8,128)(2,1)S(1)} %get-tuple-element.404), channel_id=1, source_target_pairs={{0,1},{1,2},{2,3},{3,4},{4,5},{5,6},{6,7},{7,8},{8,9},{9,10},{10,1... | collective-permute-start | bytes 6291464 | tf_op jit(solution)/shard_map/ppermute | solution.py:17
  73.4 27.6 %copy-start.67 = (f32[129]{0:T(256)}, f32[129]{0:T(256)S(1)}, u32[]{:S(2)}) copy-start(f32[129]{0:T(256)S(1)} %fusion.154) | copy-start | bytes 1552
  73.4 60.1 %copy-start.69 = (f32[129]{0:T(256)}, f32[129]{0:T(256)S(1)}, u32[]{:S(2)}) copy-start(f32[129]{0:T(256)S(1)} %fusion.151) | copy-start | bytes 1552
  75.6 25.4 %copy-start.2 = (f32[129,8192]{1,0:T(8,128)}, f32[129,8192]{1,0:T(8,128)S(1)}, u32[]{:S(2)}) copy-start(f32[129,8192]{1,0:T(8,128)S(1)} %convolution_negate_fusion.1) | copy-start | bytes 12681220
  77.9 20.7 %copy-start.3 = (f32[129,8192]{1,0:T(8,128)}, f32[129,8192]{1,0:T(8,128)S(1)}, u32[]{:S(2)}) copy-start(f32[129,8192]{1,0:T(8,128)S(1)} %fusion.5) | copy-start | bytes 12681220
  80.2 18.5 %copy-start.4 = (f32[129,8192]{1,0:T(8,128)}, f32[129,8192]{1,0:T(8,128)S(1)}, u32[]{:S(2)}) copy-start(f32[129,8192]{1,0:T(8,128)S(1)} %convolution_multiply_fusion.1) | copy-start | bytes 12681220
  128.3 22.1 %copy-start.11 = (f32[8,2048]{1,0:T(8,128)S(1)}, f32[8,2048]{1,0:T(8,128)}, u32[]{:S(2)}) copy-start(f32[8,2048]{1,0:T(8,128)} %param.17) | copy-start | bytes 196612
  128.3 22.2 %copy-start.50 = (f32[8,2048]{1,0:T(8,128)S(1)}, f32[8,2048]{1,0:T(8,128)}, u32[]{:S(2)}) copy-start(f32[8,2048]{1,0:T(8,128)} %param.18) | copy-start | bytes 196612
  136.8 183.4 %all-gather.8.cloned.1.call-start = ((), (), s32[]{:S(2)}) async-start(), calls=%async_computation.3 | async-start | bytes 4325376 | tf_op jit(solution)/shard_map/all_gather | solution.py:23
  143.8 256.6 %all-gather.6.cloned.1.call-start = ((), (), s32[]{:S(2)}) async-start(), calls=%async_computation.2 | async-start | bytes 4325376 | tf_op jit(solution)/shard_map/all_gather | solution.py:23
  150.1 328.0 %all-gather.4.cloned.1.call-start = ((), (), s32[]{:S(2)}) async-start(), calls=%async_computation.1 | async-start | bytes 11141120 | tf_op jit(solution)/shard_map/all_gather | solution.py:135
  190.0 88.8 %copy-start.68 = (f32[129]{0:T(256)S(1)}, f32[129]{0:T(256)}, u32[]{:S(2)}) copy-start(f32[129]{0:T(256)} %copy-done.67) | copy-start | bytes 1552
  239.9 38.9 %collective-permute-start.5 = (bf16[128,8192]{1,0:T(8,128)(2,1)S(1)}, bf16[128,8192]{1,0:T(8,128)(2,1)S(1)}, u32[]{:S(2)}, u32[]{:S(2)}) collective-permute-start(bf16[128,8192]{1,0:T(8,128)(2,1)S(1)} %get-tuple-element.402), channel_id=1, source_target_pairs={{1,0},{2,1},{3,2},{4,3},{5,4},{6,5},{7,6},{8,7},{9,8},{10,9},{11,1... | collective-permute-start | bytes 6291464 | tf_op jit(solution)/shard_map/ppermute | solution.py:17
  400.4 77.7 %copy-start.70 = (f32[129]{0:T(256)S(1)}, f32[129]{0:T(256)}, u32[]{:S(2)}) copy-start(f32[129]{0:T(256)} %copy-done.69) | copy-start | bytes 1552
  478.0 18.7 %copy-start.52 = (f32[1,8192]{1,0:T(1,128)S(1)}, f32[1,8192]{1,0:T(1,128)}, u32[]{:S(2)}) copy-start(f32[1,8192]{1,0:T(1,128)} %copy-done.51) | copy-start | bytes 98308
  478.0 18.7 %copy-start.54 = (f32[1,8192]{1,0:T(1,128)S(1)}, f32[1,8192]{1,0:T(1,128)}, u32[]{:S(2)}) copy-start(f32[1,8192]{1,0:T(1,128)} %copy-done.53) | copy-start | bytes 98308
  478.0 18.7 %copy-start.56 = (f32[1,8192]{1,0:T(1,128)S(1)}, f32[1,8192]{1,0:T(1,128)}, u32[]{:S(2)}) copy-start(f32[1,8192]{1,0:T(1,128)} %copy-done.55) | copy-start | bytes 98308
  478.0 18.7 %copy-start.58 = (f32[1,8192]{1,0:T(1,128)S(1)}, f32[1,8192]{1,0:T(1,128)}, u32[]{:S(2)}) copy-start(f32[1,8192]{1,0:T(1,128)} %copy-done.57) | copy-start | bytes 98308
  478.0 18.7 %copy-start.60 = (f32[1,8192]{1,0:T(1,128)S(1)}, f32[1,8192]{1,0:T(1,128)}, u32[]{:S(2)}) copy-start(f32[1,8192]{1,0:T(1,128)} %copy-done.59) | copy-start | bytes 98308
  478.1 18.7 %copy-start.62 = (f32[1,8192]{1,0:T(1,128)S(1)}, f32[1,8192]{1,0:T(1,128)}, u32[]{:S(2)}) copy-start(f32[1,8192]{1,0:T(1,128)} %get-tuple-element.438) | copy-start | bytes 98308
  478.1 18.7 %copy-start.64 = (f32[1,8192]{1,0:T(1,128)S(1)}, f32[1,8192]{1,0:T(1,128)}, u32[]{:S(2)}) copy-start(f32[1,8192]{1,0:T(1,128)} %get-tuple-element.439) | copy-start | bytes 98308
  478.1 18.7 %copy-start.66 = (f32[1,8192]{1,0:T(1,128)S(1)}, f32[1,8192]{1,0:T(1,128)}, u32[]{:S(2)}) copy-start(f32[1,8192]{1,0:T(1,128)} %get-tuple-element.440) | copy-start | bytes 98308
  478.1 53.7 %slice-start = ((s8[4456448]{0:T(1024)(128)(4,1)}), s8[4194304]{0:T(1024)(128)(4,1)S(1)}, s32[]{:S(2)}) async-start(s8[4456448]{0:T(1024)(128)(4,1)} %bitcast.139), calls=%async_computation.5 | async-start | bytes 8388608
  496.8 35.1 %slice-start.1 = ((s8[4456448]{0:T(1024)(128)(4,1)}), s8[262144]{0:T(1024)(128)(4,1)S(1)}, s32[]{:S(2)}) async-start(s8[4456448]{0:T(1024)(128)(4,1)} %bitcast.139), calls=%async_computation.6 | async-start | bytes 524288
  522.5 54.2 %collective-permute-start.4 = (bf16[6,8192]{1,0:T(8,128)(2,1)S(1)}, bf16[6,8192]{1,0:T(8,128)(2,1)S(1)}, u32[]{:S(2)}, u32[]{:S(2)}) collective-permute-start(bf16[6,8192]{1,0:T(8,128)(2,1)S(1)} %slice.766), channel_id=1, source_target_pairs={{1,0},{2,1},{3,2},{4,3},{5,4},{6,5},{7,6},{8,7},{9,8},{10,9},{11,1... | collective-permute-start | bytes 294920 | tf_op jit(solution)/shard_map/ppermute | solution.py:17
  572.8 9.3 %collective-permute-start.6 = (bf16[6,8192]{1,0:T(8,128)(2,1)S(1)}, bf16[6,8192]{1,0:T(8,128)(2,1)S(1)}, u32[]{:S(2)}, u32[]{:S(2)}) collective-permute-start(bf16[6,8192]{1,0:T(8,128)(2,1)S(1)} %slice.774), channel_id=1, source_target_pairs={{1,0},{2,1},{3,2},{4,3},{5,4},{6,5},{7,6},{8,7},{9,8},{10,9},{11,1... | collective-permute-start | bytes 294920 | tf_op jit(solution)/shard_map/ppermute | solution.py:17
  574.8 12.5 %collective-permute-start.7 = (bf16[6,8192]{1,0:T(8,128)(2,1)S(1)}, bf16[6,8192]{1,0:T(8,128)(2,1)S(1)}, u32[]{:S(2)}, u32[]{:S(2)}) collective-permute-start(bf16[6,8192]{1,0:T(8,128)(2,1)S(1)} %slice.782), channel_id=1, source_target_pairs={{1,0},{2,1},{3,2},{4,3},{5,4},{6,5},{7,6},{8,7},{9,8},{10,9},{11,1... | collective-permute-start | bytes 294920 | tf_op jit(solution)/shard_map/ppermute | solution.py:17
  (55 other events, 279.2 us)
Sparse Core Ops, SparseCore 0:
  136.9 22.8 reduce-scatter.3
Sparse Core Ops, SparseCore 1:
  143.9 66.1 all-gather.7
  212.8 65.6 all-gather.5
  279.9 67.9 all-gather.3
where the time goes:
time: 612 us; the launch traced here: 600 us
  other arithmetic  140 us (23%)
  blocking collectives  126 us (21%)
  local copies, waits for them, and re-layouts  114 us (19%)
  matrix products  114 us (19%)
  loops' own time  44.2 us (7%)
  starting transfers between devices  29 us (5%)
  between operations  17.6 us (3%)
  waiting for transfers between devices  16.1 us (3%)
    select_n x64, other arithmetic, hop(): return jax.tree.map(lambda a, b: jnp.where(reached, a, b), new, before)  70.8 us
    another operation x2, loops' own time, carried_in(): return lax.fori_loop(0, size, hop, start)  44.2 us
    unnamed x1, blocking collectives  42.1 us
    dynamic_slice x64, local copies, waits for them, and re-layouts, hop(): part[at].astype(own.dtype)  41.9 us
    dot_general x2, matrix products, restore(): jnp.dot(table_set[3], imag_part, precision=exact_mode, preferred_element_...  39.1 us
    dot_general x2, matrix products, restore(): jnp.dot(table_set[2], real_part, precision=exact_mode, preferred_element_...  35.9 us
    all_gather x1, blocking collectives, shards(): lax.all_gather(residues, 'own', axis=1, tiled=True)  35.7 us
    ppermute x8, starting transfers between devices, from_behind(): lax.ppermute(value, axis, [(source, source + steps) for source in range(l...  28.7 us
  transfers between devices with their start and end apart: 12, of which 1 were waited for; matrix products, arithmetic and copies ran while one was open for 41% of the time, Pallas kernels for 0%

commit v1 on v0

v1 whole, which is shorter than its diff:
```python
import functools
import math

import jax
import jax.numpy as jnp
from jax import lax
from jax.experimental import pallas as pl
from jax.experimental.pallas import tpu as pltpu
from jax.sharding import PartitionSpec as P

AXES = ("ctx", "own")
SUB = 8
f32, bf16 = jnp.float32, jnp.bfloat16
VMEM_LIMIT = 48 * 1024 * 1024


def from_behind(value, axis, steps):
    count = lax.axis_size(axis)
    leading, last = (max(0, -steps), min(count, count - steps))
    return lax.ppermute(value, axis, [(source, source + steps) for source in range(leading, last)])


def mm(a, b):
    return jnp.dot(a, b, preferred_element_type=f32)


def odd_tables(rows):
    odd = 2 * jnp.arange(rows, dtype=jnp.int32)[:, None] + 1
    place = jnp.arange(rows, dtype=jnp.int32)[None, :]

    def matrix(at):
        angle = ((odd * at) % (4 * rows)).astype(f32) * (math.pi / (2 * rows))
        return jnp.concatenate([jnp.cos(angle), -jnp.sin(angle)], axis=0)

    here, before = matrix(place), matrix(place + 3 * rows)
    back = here.T / rows
    return here.astype(bf16), before.astype(bf16), back.astype(bf16)


def spread_matrix(groups, width, cpg, first):
    row = lax.broadcasted_iota(jnp.int32, (groups, width), 0)
    col = lax.broadcasted_iota(jnp.int32, (groups, width), 1)
    start = (row - first) * cpg
    return jnp.logical_and(col >= start, col < start + cpg)


def conv_rows(rim, main, taps):
    rows = main.shape[0]
    joined = jnp.concatenate([rim, main], axis=0)
    total = taps[0:1] * main
    for j in range(1, taps.shape[0]):
        total = total + taps[j : j + 1] * pltpu.roll(joined, j, 0)[SUB:]
    return total


def corr_rows(main, rim, taps):
    rows = main.shape[0]
    joined = jnp.concatenate([main, rim], axis=0)
    total = taps[0:1] * main
    for j in range(1, taps.shape[0]):
        total = total + taps[j : j + 1] * pltpu.roll(joined, rows + SUB - j, 0)[:rows]
    return total


def modal_rows(coeff, decay, rows, reverse):
    poles, width = decay.shape
    step = lax.broadcasted_iota(jnp.int32, (SUB, width), 0).astype(f32)
    lag = (SUB - step) if reverse else step
    hop = jnp.exp(-float(SUB) * decay)
    now = [coeff[r : r + 1] * jnp.exp(-decay[r : r + 1] * lag) for r in range(poles)]
    hops = [jnp.broadcast_to(hop[r : r + 1], (SUB, width)) for r in range(poles)]
    parts = []
    for k in range(rows // SUB):
        total = now[0]
        for r in range(1, poles):
            total = total + now[r]
        parts.append(total)
        if k + 1 < rows // SUB:
            now = [a * b for a, b in zip(now, hops)]
    if reverse:
        parts = parts[::-1]
    return jnp.concatenate(parts, axis=0)


def block_states(x, decay, reverse):
    poles, width = decay.shape
    rows = x.shape[0]
    step = lax.broadcasted_iota(jnp.int32, (SUB, width), 0).astype(f32)
    lag = step if reverse else (SUB - 1 - step)
    hop = jnp.exp(-float(SUB) * decay)
    order = list(range(rows // SUB))
    if reverse:
        order = order[::-1]
    states = []
    for r in range(poles):
        one = jnp.broadcast_to(hop[r : r + 1], (SUB, width))
        total = x[order[0] * SUB : (order[0] + 1) * SUB]
        for k in order[1:]:
            total = total * one + x[k * SUB : (k + 1) * SUB]
        states.append(
            jnp.sum(total * jnp.exp(-decay[r : r + 1] * lag), axis=0, keepdims=True)
        )
    return jnp.concatenate(states, axis=0)


def pieces(tile, width, body):
    def step(i, carry):
        body(i, pl.ds(pl.multiple_of(i * width, width), width))
        return carry

    lax.fori_loop(0, tile // width, step, 0)


def short_of(short_ref, groups, width, cpg, i):
    spread = spread_matrix(groups, width, cpg, i * (width // cpg)).astype(f32)
    return jnp.dot(
        short_ref[...], spread, precision=lax.Precision.HIGHEST, preferred_element_type=f32
    )


def first_kernel(
    cpg, width, taps, q_ref, k_ref, v_ref, g_ref, rim_ref, short_ref, decay_ref,
    qf_ref, kf_ref, vf_ref, p_ref, gc_ref, st_ref,
):
    groups = short_ref.shape[1]

    def body(i, at):
        short = short_of(short_ref, groups, width, cpg, i)
        rim = rim_ref[:, at].astype(f32)

        def feat(n, ref):
            out = conv_rows(
                rim[n * SUB : (n + 1) * SUB],
                ref[:, at].astype(f32),
                short[n * SUB : n * SUB + taps],
            )
            return out.astype(bf16)

        qf, kf, vf = feat(0, q_ref), feat(1, k_ref), feat(2, v_ref)
        qf_ref[:, at] = qf
        kf_ref[:, at] = kf
        vf_ref[:, at] = vf
        product = (kf.astype(f32) * vf.astype(f32)).astype(bf16)
        p_ref[:, at] = product
        conv = (g_ref[:, at].astype(f32) * qf.astype(f32)).astype(bf16)
        gc_ref[:, at] = conv
        decay = decay_ref[:, at]
        poles = decay.shape[0]
        st_ref[:, at] = jnp.concatenate(
            [
                block_states(product.astype(f32), decay, False),
                block_states(conv.astype(f32), decay, True),
            ],
            axis=0,
        ).astype(bf16)

    pieces(q_ref.shape[1], width, body)


def times(a, b, rows):
    ar, ai, br, bi = a[:rows], a[rows:], b[:rows], b[rows:]
    return jnp.concatenate([ar * br - ai * bi, ar * bi + ai * br], axis=0).astype(bf16)


def times_conj(a, b, rows):
    ar, ai, br, bi = a[:rows], a[rows:], b[:rows], b[rows:]
    return jnp.concatenate([ar * br + ai * bi, ai * br - ar * bi], axis=0).astype(bf16)


def group_total(spec, groups, width, cpg, i):
    spread = spread_matrix(groups, width, cpg, i * (width // cpg)).astype(bf16)
    return lax.dot_general(
        spec, spread, (((1,), (1,)), ((), ())), preferred_element_type=f32
    )


def own_kernel(
    cpg, width, here_ref, back_ref, p_ref, gc_ref, decay_ref, weight_ref, long_ref,
    near_ref, nearb_ref, taps_ref, corr_ref,
):
    rows, tile = p_ref.shape
    groups = long_ref.shape[1]
    corr_ref[...] = jnp.zeros_like(corr_ref)

    def body(i, at):
        spread = spread_matrix(groups, width, cpg, i * (width // cpg)).astype(bf16)
        head = modal_rows(weight_ref[:, at], decay_ref[:, at], rows, False)
        head = head + mm(long_ref[...].astype(bf16), spread)
        head_spec = mm(here_ref[...], head.astype(bf16))
        own = mm(here_ref[...], p_ref[:, at])
        cur = mm(here_ref[...], gc_ref[:, at])
        near_ref[:, at] = mm(back_ref[...], times(own, head_spec, rows)).astype(bf16)
        nearb_ref[:, at] = mm(back_ref[...], times_conj(cur, head_spec, rows)).astype(bf16)
        corr_ref[...] += group_total(times_conj(cur, own, rows), groups, width, cpg, i)

    pieces(tile, width, body)
    taps_ref[...] = mm(back_ref[...], corr_ref[...].astype(bf16))


def last_kernel(
    cpg, width, taps, scale, here_ref, before_ref, back_ref, prev_ref, next_ref, gc_ref,
    near_ref, nearb_ref, qf_ref, kf_ref, vf_ref, g_ref, state_ref, decay_ref, weight_ref,
    long_ref, short_ref, tapsin_ref,
    lay_ref, gq_ref, gk_ref, gv_ref, head_ref, tail_ref, taps_ref, corr_ref, edge_ref,
):
    rows, tile = prev_ref.shape
    groups = long_ref.shape[1]
    corr_ref[...] = jnp.zeros_like(corr_ref)
    edge_ref[...] = mm(here_ref[...], long_ref[...].astype(bf16)).astype(bf16)

    def body(i, at):
        spread = spread_matrix(groups, width, cpg, i * (width // cpg)).astype(bf16)
        short = short_of(short_ref, groups, width, cpg, i)
        edge = mm(edge_ref[...], spread)
        prev = mm(before_ref[...], prev_ref[:, at])
        nxt = -mm(before_ref[...], next_ref[:, at])
        cur = mm(here_ref[...], gc_ref[:, at])
        decay, weight = decay_ref[:, at], weight_ref[:, at]
        poles = decay.shape[0]
        state = state_ref[:, at].astype(f32)
        corr_ref[...] += group_total(times_conj(cur, prev, rows), groups, width, cpg, i)
        conv = near_ref[:, at].astype(f32) + mm(back_ref[...], times(prev, edge, rows))
        conv = conv + modal_rows(
            weight * jnp.exp(-decay) * state[:poles], decay, rows, False
        )
        lay_ref[:, at] = (qf_ref[:, at].astype(f32) * conv).astype(bf16)
        grad = nearb_ref[:, at].astype(f32) + mm(back_ref[...], times_conj(nxt, edge, rows))
        grad = grad + modal_rows(weight * state[poles:], decay, rows, True)
        zero = jnp.zeros((SUB, width), f32)

        def finish(n, value, out_ref):
            value = value.astype(bf16)
            head_ref[n * SUB : (n + 1) * SUB, at] = value[:SUB]
            out = corr_rows(value.astype(f32), zero, short[n * SUB : n * SUB + taps])
            tail_ref[n * SUB : (n + 1) * SUB, at] = out[rows - SUB :]
            out_ref[:, at] = out.astype(bf16)

        finish(0, g_ref[:, at].astype(f32) * conv, gq_ref)
        finish(1, grad * vf_ref[:, at].astype(f32), gk_ref)
        finish(2, grad * kf_ref[:, at].astype(f32), gv_ref)

    pieces(tile, width, body)
    total = tapsin_ref[...] + mm(back_ref[...], corr_ref[...].astype(bf16))
    taps_ref[...] = (total * scale).astype(bf16)


def edge_kernel(cpg, width, taps, rim_ref, tail_ref, short_ref, *refs):
    olds, outs = refs[:3], refs[3:]
    groups = short_ref.shape[1]

    def body(i, at):
        short = short_of(short_ref, groups, width, cpg, i)
        for n in range(3):
            part = short[n * SUB : n * SUB + taps]
            zero = jnp.zeros((SUB, width), f32)
            rim = rim_ref[n * SUB : (n + 1) * SUB, at].astype(f32)
            add = corr_rows(zero, rim, part)
            low = tail_ref[n * SUB : (n + 1) * SUB, at] + add
            outs[n][:, at] = jnp.concatenate(
                [olds[n][:SUB, at].astype(f32), low], axis=0
            ).astype(bf16)

    pieces(tail_ref.shape[1], width, body)


def scan_kernel(x_ref, rate_ref, out_ref):
    count = x_ref.shape[0]
    poles = rate_ref.shape[0]
    keep = jnp.exp(-rate_ref[...])

    def step(k, carry):
        ahead, behind = carry
        out_ref[k, :poles] = ahead
        at = count - 1 - k
        out_ref[at, poles:] = behind
        return (
            keep * ahead + x_ref[k, :poles],
            keep * behind + x_ref[at, poles:],
        )

    zero = jnp.zeros(keep.shape, f32)
    lax.fori_loop(0, count, step, (zero, zero))


def params():
    return pltpu.CompilerParams(vmem_limit_bytes=VMEM_LIMIT)


def shards(query_proj, key_proj, value_proj, short_taps, long_taps, decay_rate, residues, grad_out):
    rows, chans = query_proj.shape
    owners = lax.axis_size("own")
    count = owners * lax.axis_size("ctx")
    tap_count = short_taps.shape[1]
    groups_own = short_taps.shape[2]
    groups = groups_own * owners
    cpg = chans // groups
    poles = decay_rate.shape[0]
    tile = groups_own * cpg
    steps = chans // tile
    width = 256
    shape = jax.ShapeDtypeStruct

    rims = from_behind(
        jnp.concatenate([query_proj[-SUB:], key_proj[-SUB:], value_proj[-SUB:]], axis=0), AXES, 1
    )
    short_pad = jnp.pad(short_taps, ((0, 0), (0, SUB - tap_count), (0, 0))).reshape(
        3 * SUB, groups_own
    )
    weight_own = residues * jnp.sqrt(-jnp.expm1(-2.0 * decay_rate))
    short_all = lax.all_gather(short_pad, "own", axis=1, tiled=True)
    modal_all = lax.all_gather(
        jnp.concatenate([decay_rate, weight_own], axis=0), "own", axis=1, tiled=True
    )
    long_all = lax.all_gather(long_taps, "own", axis=1, tiled=True)
    decay_all, weight_all = modal_all[:poles], modal_all[poles:]
    here, before, back = odd_tables(rows)

    def cols(height, wide=tile):
        return pl.BlockSpec((height, wide), lambda i: (0, i))

    def whole(height, wide):
        return pl.BlockSpec((height, wide), lambda i: (0, 0))

    big = shape((rows, chans), bf16)
    qf, kf, vf, product, conv, states = pl.pallas_call(
        functools.partial(first_kernel, cpg, width, tap_count),
        grid=(steps,),
        in_specs=[cols(rows)] * 4 + [cols(3 * SUB), cols(3 * SUB, groups_own), cols(poles)],
        out_specs=[cols(rows)] * 5 + [cols(2 * poles)],
        out_shape=[big] * 5 + [shape((2 * poles, chans), bf16)],
        compiler_params=params(),
        cost_estimate=pl.CostEstimate(
            flops=100 * rows * chans, bytes_accessed=18 * rows * chans, transcendentals=0
        ),
        name="first",
    )(query_proj, key_proj, value_proj, grad_out, rims, short_all, decay_all)

    earlier = from_behind(product, AXES, 1)
    later = from_behind(conv, AXES, -1)

    part = chans // count
    sent = states.reshape(2 * poles, count, part).transpose(1, 0, 2)
    got = lax.all_to_all(sent, AXES, 0, 0, tiled=True).astype(f32)
    me = lax.axis_index("ctx") * owners + lax.axis_index("own")
    rate = lax.dynamic_slice_in_dim(decay_all, me * part, part, 1) * float(rows)
    scanned = pl.pallas_call(
        scan_kernel, out_shape=shape((count, 2 * poles, part), f32), name="scan"
    )(got, rate)
    returned = lax.all_to_all(scanned.astype(bf16), AXES, 0, 0, tiled=True)
    state_in = returned.transpose(1, 0, 2).reshape(2 * poles, chans)

    near, near_back, taps_own = pl.pallas_call(
        functools.partial(own_kernel, cpg, width),
        grid=(steps,),
        in_specs=[
            whole(2 * rows, rows), whole(rows, 2 * rows), cols(rows), cols(rows),
            cols(poles), cols(poles), cols(long_taps.shape[0], groups_own),
        ],
        out_specs=[cols(rows), cols(rows), cols(rows, groups_own)],
        out_shape=[big, big, shape((rows, groups), f32)],
        scratch_shapes=[pltpu.VMEM((2 * rows, groups_own), f32)],
        compiler_params=params(),
        cost_estimate=pl.CostEstimate(
            flops=14 * rows * rows * chans, bytes_accessed=8 * rows * chans, transcendentals=0
        ),
        name="own",
    )(here, back, product, conv, decay_all, weight_all, long_all)

    scale = 1.0 / math.sqrt(rows * count * cpg)
    layer_out, gq, gk, gv, heads, tails, taps_part = pl.pallas_call(
        functools.partial(last_kernel, cpg, width, tap_count, scale),
        grid=(steps,),
        in_specs=[whole(2 * rows, rows), whole(2 * rows, rows), whole(rows, 2 * rows)]
        + [cols(rows)] * 9
        + [
            cols(2 * poles), cols(poles), cols(poles), cols(long_taps.shape[0], groups_own),
            cols(3 * SUB, groups_own), cols(rows, groups_own),
        ],
        out_specs=[cols(rows)] * 4 + [cols(3 * SUB), cols(3 * SUB), cols(rows, groups_own)],
        out_shape=[big] * 4
        + [
            shape((3 * SUB, chans), bf16), shape((3 * SUB, chans), f32),
            shape((rows, groups), bf16),
        ],
        scratch_shapes=[
            pltpu.VMEM((2 * rows, groups_own), f32), pltpu.VMEM((2 * rows, groups_own), bf16)
        ],
        compiler_params=params(),
        cost_estimate=pl.CostEstimate(
            flops=16 * rows * rows * chans, bytes_accessed=26 * rows * chans, transcendentals=0
        ),
        name="last",
    )(
        here, before, back, earlier, later, conv, near, near_back, qf, kf, vf, grad_out,
        state_in, decay_all, weight_all, long_all, short_all, taps_own,
    )

    rim_after = from_behind(heads, AXES, -1)
    bottom = pl.BlockSpec((2 * SUB, tile), lambda i: (rows // (2 * SUB) - 1, i))
    gq, gk, gv = pl.pallas_call(
        functools.partial(edge_kernel, cpg, width, tap_count),
        grid=(steps,),
        in_specs=[cols(3 * SUB), cols(3 * SUB), cols(3 * SUB, groups_own)] + [bottom] * 3,
        out_specs=[bottom] * 3,
        out_shape=[big] * 3,
        input_output_aliases={3: 0, 4: 1, 5: 2},
        compiler_params=params(),
        name="edge",
    )(rim_after, tails, short_all, gq, gk, gv)

    owned = lax.psum_scatter(taps_part, "own", scatter_dimension=1, tiled=True)
    grad_taps = lax.psum(owned, "ctx").astype(f32)
    return (layer_out, gq, gk, gv, grad_taps)


def solution(mesh):
    block = P(AXES, None)
    return jax.shard_map(
        shards,
        mesh=mesh,
        in_specs=(
            block, block, block, P(None, None, "own"), P(None, "own"), P(None, "own"),
            P(None, "own"), block,
        ),
        out_specs=(block, block, block, block, P(None, "own")),
        check_vma=False,
    )
```

time: 612 us -> 278 us (0.45)
  the two profiles are of different devices: /device:TPU:1 before, /device:TPU:0 now
where the time goes in v1:
time: 278 us; the launch traced here: 277 us
  Pallas kernels  99.1 us (36%)
  blocking collectives  59 us (21%)
  waiting for transfers between devices  48.7 us (18%)
  starting transfers between devices  36.1 us (13%)
  between operations  14.2 us (5%)
  local copies, waits for them, and re-layouts  13.8 us (5%)
  other arithmetic  6.28 us (2%)
    pallas_call x1, Pallas kernels, shards(): pl.pallas_call(functools.partial(last_kernel, cpg, width, tap_count, scal...  38.9 us
    psum x1, blocking collectives, shards(): grad_taps = lax.psum(owned, 'ctx').astype(f32)  37.1 us
    all_to_all x1, waiting for transfers between devices, shards(): got = lax.all_to_all(sent, AXES, 0, 0, tiled=True).astype(f32)  27.2 us
    pallas_call x1, Pallas kernels, shards(): pl.pallas_call(functools.partial(first_kernel, cpg, width, tap_count), gr...  27.1 us
    pallas_call x1, Pallas kernels, shards(): pl.pallas_call(functools.partial(own_kernel, cpg, width), grid=(steps,),...  22.2 us
    unnamed x2, waiting for transfers between devices  21.5 us
    all_to_all x1, starting transfers between devices, shards(): returned = lax.all_to_all(scanned.astype(bf16), AXES, 0, 0, tiled=True)  18.8 us
    all_to_all x1, starting transfers between devices, shards(): got = lax.all_to_all(sent, AXES, 0, 0, tiled=True).astype(f32)  9.96 us
  transfers between devices with their start and end apart: 7, of which 2 were waited for; matrix products, arithmetic and copies ran while one was open for 4% of the time, Pallas kernels for 9%

profile of v1, /device:TPU:0, one launch (start us, length us, event | category | flops | bytes accessed | tf_op | source)
XLA Modules:
  0.0 277.1 jit_solution(10083520485786414746)
XLA Ops:
  7.2 0.9 slice.15
  8.1 0.9 slice.16
  9.0 0.9 slice.17
  10.0 2.4 collective-permute-start
  12.4 0.9 sqrt_multiply_fusion
  13.3 0.9 pad_maximum_fusion.2
  14.1 9.6 %all_gather.10 = f32[16,8192]{1,0:T(8,128)S(1)} all-gather(f32[16,2048]{1,0:T(8,128)S(1)} %pad_maximum_fusion.2), channel_id=1, replica_groups=mesh['ctx'=8,'own'=4] {'own'}, dimensions={1}, use_global_device_ids=true | all-gather | bytes 655360 | tf_op jit(solution)/shard_map/all_gather | solution.py:311
  23.8 5.2 %all_gather.9.short_ref = f32[24,512]{1,0:T(8,128)S(1)} all-gather(f32[24,128]{1,0:T(8,128)S(1)} %pad_bitcast_fusion), channel_id=1, replica_groups=mesh['ctx'=8,'own'=4] {'own'}, dimensions={1}, use_global_device_ids=true | all-gather | bytes 61440 | tf_op jit(solution)/shard_map/all_gather | solution.py:310
  29.0 27.1 %first.1 = (bf16[128,8192]{1,0:T(8,128)(2,1)S(1)}, bf16[128,8192]{1,0:T(8,128)(2,1)S(1)}, bf16[128,8192]{1,0:T(8,128)(2,1)}, bf16[128,8192]{1,0:T(8,128)(2,1)}, ...) custom-call(bf16[128,8192]{1,0:T(8,128)(2,1)} %q_ref.1, bf16[128,8192]{1,0:T(8,128)(2,1)} %k_ref.1, ...), custom_call_target="tpu_custom_call" | custom-call | flops 104857600 | bytes 18874368 | tf_op jit(solution)/shard_map/first/pallas_call | solution.py:325
  56.1 1.4 copy-done
  57.4 1.4 copy-done.1
  58.8 2.4 collective-permute-start.1
  61.2 1.3 collective-permute-start.2
  63.2 10.0 %all-to-all-start = ((bf16[32,16,256]{2,1,0:T(8,128)(2,1)}), bf16[32,16,256]{2,1,0:T(8,128)(2,1)S(1)}, u32[]{:S(2)}, u32[]{:S(2)}) async-start(bf16[32,16,256]{2,1,0:T(8,128)(2,1)} %bitcast.15), calls=%async_computation | async-start | bytes 524288 | tf_op jit(solution)/shard_map/all_to_all | solution.py:343
  73.8 27.2 %all-to-all-done = bf16[32,16,256]{2,1,0:T(8,128)(2,1)S(1)} async-done(((bf16[32,16,256]{2,1,0:T(8,128)(2,1)}), bf16[32,16,256]{2,1,0:T(8,128)(2,1)S(1)}, u32[]{:S(2)}, u32[]{:S(2)}) %all-to-all-start) | async-done | bytes 262176 | tf_op jit(solution)/shard_map/all_to_all | solution.py:343
  101.0 0.9 convert_element_type.35.x_ref
  101.8 2.1 scan.1
  103.9 1.8 convert_element_type.36
  105.7 18.8 %all-to-all-start.1 = ((bf16[32,16,256]{2,1,0:T(8,128)(2,1)}), bf16[32,16,256]{2,1,0:T(8,128)(2,1)}, u32[]{:S(2)}, u32[]{:S(2)}) async-start(bf16[32,16,256]{2,1,0:T(8,128)(2,1)} %convert_element_type.36), calls=%async_computation.1 | async-start | bytes 524288 | tf_op jit(solution)/shard_map/all_to_all | solution.py:349
  125.3 7.1 %all_gather.11.long_ref = f32[128,512]{1,0:T(8,128)S(1)} all-gather(f32[128,128]{1,0:T(8,128)S(1)} %copy-done.6), channel_id=1, replica_groups=mesh['ctx'=8,'own'=4] {'own'}, dimensions={1}, use_global_device_ids=true | all-gather | bytes 327680 | tf_op jit(solution)/shard_map/all_gather | solution.py:314
  132.4 22.2 %own.1 = (bf16[128,8192]{1,0:T(8,128)(2,1)S(1)}, bf16[128,8192]{1,0:T(8,128)(2,1)S(1)}, f32[128,512]{1,0:T(8,128)S(1)}) custom-call(bf16[256,128]{1,0:T(8,128)(2,1)S(1)} %copy.28.here_ref, bf16[128,256]{1,0:T(8,128)(2,1)S(1)} %fusion.7.back_ref, bf16[128,8192]{1,0:T(8,128)(2,1)} %get-tuple-element.24.p_ref, bf16[128,8192]{1,0:T(8,128)(2,1)} %get-tuple-element.25.gc_ref, ...), custom_call_target="tpu_custom_call" | custom-call | flops 1879048192 | bytes 8388608 | tf_op jit(solution)/shard_map/own/pallas_call | solution.py:352
  154.7 1.3 copy-done.2
  156.0 1.3 copy-done.3
  157.4 1.0 copy.33
  158.4 38.9 %last.1 = (bf16[128,8192]{1,0:T(8,128)(2,1)}, bf16[128,8192]{1,0:T(8,128)(2,1)}, bf16[128,8192]{1,0:T(8,128)(2,1)}, bf16[128,8192]{1,0:T(8,128)(2,1)}, bf16[24,8...) custom-call(bf16[256,128]{1,0:T(8,128)(2,1)S(1)} %copy.28.here_ref, ...), custom_call_target="tpu_custom_call" | custom-call | flops 2147483648 | bytes 27262976 | tf_op jit(solution)/shard_map/last/pallas_call | solution.py:370
  197.3 0.9 copy-done.4
  198.1 1.3 collective-permute-start.3
  200.2 21.5 %reduce-scatter.4.cloned.1.call-done = bf16[128,128]{1,0:T(8,128)(2,1)} async-done(((bf16[512,128]{1,0:T(8,128)(2,1)}), bf16[128,128]{1,0:T(8,128)(2,1)}) %reduce-scatter.4.cloned.1.call-update) | async-done | bytes 32784
  221.7 0.9 copy.31
  222.6 37.1 %psum.7 = bf16[128,128]{1,0:T(8,128)(2,1)S(1)} all-reduce(bf16[128,128]{1,0:T(8,128)(2,1)S(1)} %copy.31), channel_id=1, replica_groups=mesh['ctx'=8,'own'=4] {'ctx'}, use_global_device_ids=true, to_apply=%region_1.2 | all-reduce | flops 16384 | bytes 65536 | tf_op jit(solution)/shard_map/psum | solution.py:412
  260.3 1.1 copy-done.5
  261.4 8.9 %edge.1 = (bf16[128,8192]{1,0:T(8,128)(2,1)}, bf16[128,8192]{1,0:T(8,128)(2,1)}, bf16[128,8192]{1,0:T(8,128)(2,1)}) custom-call(bf16[24,8192]{1,0:T(8,128)(2,1)S(1)} %collective-permute-done.3.rim_ref, f32[24,8192]{1,0:T(8,128)S(1)} %copy-done.5, f32[24,512]{1,0:T(8,128)S(1)} %all_gather.9.short_ref, ...), custom_call_target="tpu_custom_call", output_to_operand_aliasing={{0}: (3, {}), {1}: (4, {}), {2}: (5, {})} | custom-call | tf_op jit(solution)/shard_map/edge/pallas_call | solution.py:400
  (31 shorter events, 3.7 us)
Async XLA Ops:
  7.2 16.6 %copy-start.7 = (f32[3,7,128]{2,1,0:T(8,128)S(1)}, f32[3,7,128]{2,1,0:T(8,128)}, u32[]{:S(2)}) copy-start(f32[3,7,128]{2,1,0:T(8,128)} %param.11) | copy-start | bytes 32260
  10.0 19.0 %collective-permute-start = (bf16[24,8192]{1,0:T(8,128)(2,1)S(1)}, bf16[24,8192]{1,0:T(8,128)(2,1)S(1)}, u32[]{:S(2)}, u32[]{:S(2)}) collective-permute-start(bf16[24,8192]{1,0:T(8,128)(2,1)S(1)} %pad_maximum_fusion), channel_id=1, source_target_pairs={{0,1},{1,2},{2,3},{3,4},{4,5},{5,6},{6,7},{7,8},{8,9},{9,10},{10,1... | collective-permute-start | bytes 1179656 | tf_op jit(solution)/shard_map/ppermute | solution.py:20
  56.1 1.4 copy-start
  57.4 1.4 copy-start.1
  58.8 99.5 %collective-permute-start.1 = (bf16[128,8192]{1,0:T(8,128)(2,1)}, bf16[128,8192]{1,0:T(8,128)(2,1)S(1)}, u32[]{:S(2)}, u32[]{:S(2)}) collective-permute-start(bf16[128,8192]{1,0:T(8,128)(2,1)} %get-tuple-element.24.p_ref), channel_id=1, source_target_pairs={{0,1},{1,2},{2,3},{3,4},{4,5},{5,6},{6,7},{7,8},{8,9},{9,10},{10,1... | collective-permute-start | bytes 6291464 | tf_op jit(solution)/shard_map/ppermute | solution.py:20
  61.2 97.2 %collective-permute-start.2 = (bf16[128,8192]{1,0:T(8,128)(2,1)}, bf16[128,8192]{1,0:T(8,128)(2,1)}, u32[]{:S(2)}, u32[]{:S(2)}) collective-permute-start(bf16[128,8192]{1,0:T(8,128)(2,1)} %get-tuple-element.25.gc_ref), channel_id=1, source_target_pairs={{1,0},{2,1},{3,2},{4,3},{5,4},{6,5},{7,6},{8,7},{9,8},{10,9},{11,1... | collective-permute-start | bytes 6291464 | tf_op jit(solution)/shard_map/ppermute | solution.py:20
  63.2 37.8 %all-to-all-start = ((bf16[32,16,256]{2,1,0:T(8,128)(2,1)}), bf16[32,16,256]{2,1,0:T(8,128)(2,1)S(1)}, u32[]{:S(2)}, u32[]{:S(2)}) async-start(bf16[32,16,256]{2,1,0:T(8,128)(2,1)} %bitcast.15), calls=%async_computation | async-start | bytes 524288 | tf_op jit(solution)/shard_map/all_to_all | solution.py:343
  73.2 52.2 %copy-start.6 = (f32[128,128]{1,0:T(8,128)S(1)}, f32[128,128]{1,0:T(8,128)}, u32[]{:S(2)}) copy-start(f32[128,128]{1,0:T(8,128)} %param.12) | copy-start | bytes 196612
  105.7 51.7 %all-to-all-start.1 = ((bf16[32,16,256]{2,1,0:T(8,128)(2,1)}), bf16[32,16,256]{2,1,0:T(8,128)(2,1)}, u32[]{:S(2)}, u32[]{:S(2)}) async-start(bf16[32,16,256]{2,1,0:T(8,128)(2,1)} %convert_element_type.36), calls=%async_computation.1 | async-start | bytes 524288 | tf_op jit(solution)/shard_map/all_to_all | solution.py:349
  124.4 97.3 %reduce-scatter.4.cloned.1.call-start = ((), (), s32[]{:S(2)}) async-start(), calls=%async_computation.3 | async-start | bytes 163840
  154.7 1.3 copy-start.2
  156.0 1.3 copy-start.3
  197.2 0.9 copy-start.4
  198.1 62.2 %collective-permute-start.3 = (bf16[24,8192]{1,0:T(8,128)(2,1)}, bf16[24,8192]{1,0:T(8,128)(2,1)S(1)}, u32[]{:S(2)}, u32[]{:S(2)}) collective-permute-start(bf16[24,8192]{1,0:T(8,128)(2,1)} %get-tuple-element.34), channel_id=1, source_target_pairs={{1,0},{2,1},{3,2},{4,3},{5,4},{6,5},{7,6},{8,7},{9,8},{10,9},{11,1... | collective-permute-start | bytes 1179656 | tf_op jit(solution)/shard_map/ppermute | solution.py:20
  260.3 1.1 copy-start.5
Sparse Core Ops, SparseCore 0:
  200.3 21.3 reduce-scatter.3

commit v2 on v1

--- a/solution.py
+++ b/solution.py
@@ -112,20 +112,160 @@
 
 
 def short_of(short_ref, groups, width, cpg, i):
-    spread = spread_matrix(groups, width, cpg, i * (width // cpg)).astype(f32)
-    return jnp.dot(
-        short_ref[...], spread, precision=lax.Precision.HIGHEST, preferred_element_type=f32
-    )
+    spread = spread_matrix(groups, width, cpg, i * (width // cpg)).astype(bf16)
+    value = short_ref[...]
+    count = value.shape[0]
+    high = value.astype(bf16).astype(f32)
+    both = mm(jnp.concatenate([high, value - high], axis=0).astype(bf16), spread)
+    return both[:count] + both[count:]
+
+
+def device_of(flat, owners):
+    return (lax.div(flat, owners), lax.rem(flat, owners))
+
+
+def put(src, dst, send, recv, device):
+    return pltpu.make_async_remote_copy(
+        src_ref=src,
+        dst_ref=dst,
+        send_sem=send,
+        recv_sem=recv,
+        device_id=device,
+        device_id_type=pl.DeviceIdType.MESH,
+    )
+
+
+def loop(count, body):
+    def step(k, carry):
+        body(k)
+        return carry
+
+    lax.fori_loop(1, count, step, 0)
+
+
+def greet(count, device):
+    barrier = pltpu.get_barrier_semaphore()
+    loop(
+        count,
+        lambda k: pl.semaphore_signal(
+            barrier, inc=1, device_id=device(k), device_id_type=pl.DeviceIdType.MESH
+        ),
+    )
+    pl.semaphore_wait(barrier, count - 1)
+
+
+def gather_kernel(owners, first_ref, second_ref, first_out, second_out, send, recv):
+    ctx, own = lax.axis_index("ctx"), lax.axis_index("own")
+
+    def device(k):
+        return (ctx, lax.rem(own + k, owners))
+
+    greet(owners, device)
+
+    def copies(k):
+        return [
+            put(src, dst.at[own], send.at[n, k], recv.at[n, k], device(k))
+            for n, (src, dst) in enumerate(((first_ref, first_out), (second_ref, second_out)))
+        ]
+
+    loop(owners, lambda k: [c.start() for c in copies(k)] and None)
+    first_out[own] = first_ref[...]
+    second_out[own] = second_ref[...]
+    loop(owners, lambda k: [c.wait() for c in copies(k)] and None)
+
+
+def exchange_kernel(
+    owners, count, st_ref, rate_ref, w_ref, l_ref, ret_ref, w_out, l_out,
+    got, work, scanned, send, recv, gsend, grecv,
+):
+    ctx, own = lax.axis_index("ctx"), lax.axis_index("own")
+    me = ctx * owners + own
+    poles = rate_ref.shape[0]
+
+    def device(k):
+        return device_of(lax.rem(me + k, count), owners)
+
+    greet(count, device)
+
+    def out_copy(k):
+        to = lax.rem(me + k, count)
+        return put(st_ref.at[to], got.at[me], send.at[0, k], recv.at[0, k], device(k))
+
+    def back_copy(k):
+        to = lax.rem(me + k, count)
+        return put(scanned.at[to], ret_ref.at[me], send.at[1, k], recv.at[1, k], device(k))
+
+    def gathers(k):
+        peer = (ctx, lax.rem(own + k, owners))
+        return [
+            put(src, dst.at[own], gsend.at[n, k], grecv.at[n, k], peer)
+            for n, (src, dst) in enumerate(((w_ref, w_out), (l_ref, l_out)))
+        ]
+
+    loop(count, lambda k: out_copy(k).start())
+    loop(owners, lambda k: [c.start() for c in gathers(k)] and None)
+    got[me] = st_ref[me]
+    w_out[own] = w_ref[...]
+    l_out[own] = l_ref[...]
+    loop(count, lambda k: out_copy(k).wait())
+    keep = jnp.exp(-rate_ref[...])
+
+    def step(k, carry):
+        ahead, behind = carry
+        at = count - 1 - k
+        work[k, :poles] = ahead
+        work[at, poles:] = behind
+        return (
+            keep * ahead + got[k].astype(f32)[:poles],
+            keep * behind + got[at].astype(f32)[poles:],
+        )
+
+    zero = jnp.zeros(keep.shape, f32)
+    lax.fori_loop(0, count, step, (zero, zero))
+    scanned[...] = work[...].astype(bf16)
+    loop(count, lambda k: back_copy(k).start())
+    ret_ref[me] = scanned[me]
+    loop(count, lambda k: back_copy(k).wait())
+    loop(owners, lambda k: [c.wait() for c in gathers(k)] and None)
+
+
+def reduce_kernel(owners, count, part_ref, out_ref, got, send, recv, asend, arecv):
+    ctx, own = lax.axis_index("ctx"), lax.axis_index("own")
+    me = ctx * owners + own
+    ctxs = count // owners
+
+    def device(k):
+        return device_of(lax.rem(me + k, count), owners)
+
+    greet(count, device)
+
+    def out_copy(k):
+        to = lax.rem(me + k, count)
+        return put(part_ref.at[to], got.at[me], send.at[k], recv.at[k], device(k))
+
+    def all_copy(k):
+        return put(
+            out_ref.at[ctx], out_ref.at[ctx], asend.at[k], arecv.at[k],
+            (lax.rem(ctx + k, ctxs), own),
+        )
+
+    loop(count, lambda k: out_copy(k).start())
+    got[me] = part_ref[me]
+    loop(count, lambda k: out_copy(k).wait())
+    out_ref[ctx] = jnp.sum(got[...], axis=0)
+    loop(ctxs, lambda k: all_copy(k).start())
+    loop(ctxs, lambda k: all_copy(k).wait())
 
 
 def first_kernel(
     cpg, width, taps, q_ref, k_ref, v_ref, g_ref, rim_ref, short_ref, decay_ref,
-    qf_ref, kf_ref, vf_ref, p_ref, gc_ref, st_ref,
+    qf_ref, kf_ref, vf_ref, p_ref, gc_ref, st_ref, sc_ref,
 ):
     groups = short_ref.shape[1]
 
     def body(i, at):
         short = short_of(short_ref, groups, width, cpg, i)
+        sc_ref[:, at] = short
         rim = rim_ref[:, at].astype(f32)
 
         def feat(n, ref):
@@ -185,7 +325,7 @@
     def body(i, at):
         spread = spread_matrix(groups, width, cpg, i * (width // cpg)).astype(bf16)
         head = modal_rows(weight_ref[:, at], decay_ref[:, at], rows, False)
-        head = head + mm(long_ref[...].astype(bf16), spread)
+        head = head + mm(long_ref[...], spread)
         head_spec = mm(here_ref[...], head.astype(bf16))
         own = mm(here_ref[...], p_ref[:, at])
         cur = mm(here_ref[...], gc_ref[:, at])
@@ -206,11 +346,11 @@
     rows, tile = prev_ref.shape
     groups = long_ref.shape[1]
     corr_ref[...] = jnp.zeros_like(corr_ref)
-    edge_ref[...] = mm(here_ref[...], long_ref[...].astype(bf16)).astype(bf16)
+    edge_ref[...] = mm(here_ref[...], long_ref[...]).astype(bf16)
 
     def body(i, at):
         spread = spread_matrix(groups, width, cpg, i * (width // cpg)).astype(bf16)
-        short = short_of(short_ref, groups, width, cpg, i)
+        short = short_ref[:, at]
         edge = mm(edge_ref[...], spread)
         prev = mm(before_ref[...], prev_ref[:, at])
         nxt = -mm(before_ref[...], next_ref[:, at])
@@ -241,15 +381,14 @@
 
     pieces(tile, width, body)
     total = tapsin_ref[...] + mm(back_ref[...], corr_ref[...].astype(bf16))
-    taps_ref[...] = (total * scale).astype(bf16)
+    taps_ref[...] = total * scale
 
 
 def edge_kernel(cpg, width, taps, rim_ref, tail_ref, short_ref, *refs):
     olds, outs = refs[:3], refs[3:]
-    groups = short_ref.shape[1]
 
     def body(i, at):
-        short = short_of(short_ref, groups, width, cpg, i)
+        short = short_ref[:, at]
         for n in range(3):
             part = short[n * SUB : n * SUB + taps]
             zero = jnp.zeros((SUB, width), f32)
@@ -263,27 +402,14 @@
     pieces(tail_ref.shape[1], width, body)
 
 
-def scan_kernel(x_ref, rate_ref, out_ref):
-    count = x_ref.shape[0]
-    poles = rate_ref.shape[0]
-    keep = jnp.exp(-rate_ref[...])
-
-    def step(k, carry):
-        ahead, behind = carry
-        out_ref[k, :poles] = ahead
-        at = count - 1 - k
-        out_ref[at, poles:] = behind
-        return (
-            keep * ahead + x_ref[k, :poles],
-            keep * behind + x_ref[at, poles:],
-        )
-
-    zero = jnp.zeros(keep.shape, f32)
-    lax.fori_loop(0, count, step, (zero, zero))
-
-
 def params():
     return pltpu.CompilerParams(vmem_limit_bytes=VMEM_LIMIT)
+
+
+def remote(ident):
+    return pltpu.CompilerParams(
+        vmem_limit_bytes=VMEM_LIMIT, collective_id=ident, has_side_effects=True
+    )
 
 
 def shards(query_proj, key_proj, value_proj, short_taps, long_taps, decay_rate, residues, grad_out):
@@ -299,6 +425,7 @@
     steps = chans // tile
     width = 256
     shape = jax.ShapeDtypeStruct
+    vmem = pl.BlockSpec(memory_space=pltpu.VMEM)
 
     rims = from_behind(
         jnp.concatenate([query_proj[-SUB:], key_proj[-SUB:], value_proj[-SUB:]], axis=0), AXES, 1
@@ -307,27 +434,36 @@
         3 * SUB, groups_own
     )
     weight_own = residues * jnp.sqrt(-jnp.expm1(-2.0 * decay_rate))
-    short_all = lax.all_gather(short_pad, "own", axis=1, tiled=True)
-    modal_all = lax.all_gather(
-        jnp.concatenate([decay_rate, weight_own], axis=0), "own", axis=1, tiled=True
-    )
-    long_all = lax.all_gather(long_taps, "own", axis=1, tiled=True)
-    decay_all, weight_all = modal_all[:poles], modal_all[poles:]
+    short_all, decay_all = pl.pallas_call(
+        functools.partial(gather_kernel, owners),
+        in_specs=[vmem] * 2,
+        out_specs=[vmem] * 2,
+        out_shape=[
+            shape((owners,) + short_pad.shape, f32), shape((owners,) + decay_rate.shape, f32)
+        ],
+        scratch_shapes=[pltpu.SemaphoreType.DMA((2, owners))] * 2,
+        compiler_params=remote(0),
+        name="gather",
+    )(short_pad, decay_rate)
     here, before, back = odd_tables(rows)
 
     def cols(height, wide=tile):
         return pl.BlockSpec((height, wide), lambda i: (0, i))
 
+    def owned(height, wide):
+        return pl.BlockSpec((None, height, wide), lambda i: (i, 0, 0))
+
     def whole(height, wide):
         return pl.BlockSpec((height, wide), lambda i: (0, 0))
 
     big = shape((rows, chans), bf16)
-    qf, kf, vf, product, conv, states = pl.pallas_call(
+    qf, kf, vf, product, conv, states, short_chan = pl.pallas_call(
         functools.partial(first_kernel, cpg, width, tap_count),
         grid=(steps,),
-        in_specs=[cols(rows)] * 4 + [cols(3 * SUB), cols(3 * SUB, groups_own), cols(poles)],
-        out_specs=[cols(rows)] * 5 + [cols(2 * poles)],
-        out_shape=[big] * 5 + [shape((2 * poles, chans), bf16)],
+        in_specs=[cols(rows)] * 4 + [cols(3 * SUB), owned(3 * SUB, groups_own), owned(poles, tile)],
+        out_specs=[cols(rows)] * 5 + [cols(2 * poles), cols(3 * SUB)],
+        out_shape=[big] * 5
+        + [shape((2 * poles, chans), bf16), shape((3 * SUB, chans), f32)],
         compiler_params=params(),
         cost_estimate=pl.CostEstimate(
             flops=100 * rows * chans, bytes_accessed=18 * rows * chans, transcendentals=0
@@ -340,13 +476,29 @@
 
     part = chans // count
     sent = states.reshape(2 * poles, count, part).transpose(1, 0, 2)
-    got = lax.all_to_all(sent, AXES, 0, 0, tiled=True).astype(f32)
     me = lax.axis_index("ctx") * owners + lax.axis_index("own")
-    rate = lax.dynamic_slice_in_dim(decay_all, me * part, part, 1) * float(rows)
-    scanned = pl.pallas_call(
-        scan_kernel, out_shape=shape((count, 2 * poles, part), f32), name="scan"
-    )(got, rate)
-    returned = lax.all_to_all(scanned.astype(bf16), AXES, 0, 0, tiled=True)
+    at_owner = lax.div(me * part, tile)
+    rate = lax.dynamic_slice(
+        decay_all, (at_owner, 0, me * part - at_owner * tile), (1, poles, part)
+    )[0] * float(rows)
+    slab = (count, 2 * poles, part)
+    returned, weight_all, long_all = pl.pallas_call(
+        functools.partial(exchange_kernel, owners, count),
+        in_specs=[vmem] * 4,
+        out_specs=[vmem] * 3,
+        out_shape=[
+            shape(slab, bf16),
+            shape((owners,) + weight_own.shape, f32),
+            shape((owners,) + long_taps.shape, bf16),
+        ],
+        scratch_shapes=[
+            pltpu.VMEM(slab, bf16), pltpu.VMEM(slab, f32), pltpu.VMEM(slab, bf16),
+            pltpu.SemaphoreType.DMA((2, count)), pltpu.SemaphoreType.DMA((2, count)),
+            pltpu.SemaphoreType.DMA((2, owners)), pltpu.SemaphoreType.DMA((2, owners)),
+        ],
+        compiler_params=remote(1),
+        name="exchange",
+    )(sent, rate, weight_own, long_taps.astype(bf16))
     state_in = returned.transpose(1, 0, 2).reshape(2 * poles, chans)
 
     near, near_back, taps_own = pl.pallas_call(
@@ -354,7 +506,7 @@
         grid=(steps,),
         in_specs=[
             whole(2 * rows, rows), whole(rows, 2 * rows), cols(rows), cols(rows),
-            cols(poles), cols(poles), cols(long_taps.shape[0], groups_own),
+            owned(poles, tile), owned(poles, tile), owned(long_taps.shape[0], groups_own),
         ],
         out_specs=[cols(rows), cols(rows), cols(rows, groups_own)],
         out_shape=[big, big, shape((rows, groups), f32)],
@@ -373,14 +525,14 @@
         in_specs=[whole(2 * rows, rows), whole(2 * rows, rows), whole(rows, 2 * rows)]
         + [cols(rows)] * 9
         + [
-            cols(2 * poles), cols(poles), cols(poles), cols(long_taps.shape[0], groups_own),
-            cols(3 * SUB, groups_own), cols(rows, groups_own),
+            cols(2 * poles), owned(poles, tile), owned(poles, tile),
+            owned(long_taps.shape[0], groups_own), cols(3 * SUB), cols(rows, groups_own),
         ],
         out_specs=[cols(rows)] * 4 + [cols(3 * SUB), cols(3 * SUB), cols(rows, groups_own)],
         out_shape=[big] * 4
         + [
             shape((3 * SUB, chans), bf16), shape((3 * SUB, chans), f32),
-            shape((rows, groups), bf16),
+            shape((rows, groups), f32),
         ],
         scratch_shapes=[
             pltpu.VMEM((2 * rows, groups_own), f32), pltpu.VMEM((2 * rows, groups_own), bf16)
@@ -392,7 +544,7 @@
         name="last",
     )(
         here, before, back, earlier, later, conv, near, near_back, qf, kf, vf, grad_out,
-        state_in, decay_all, weight_all, long_all, short_all, taps_own,
+        state_in, decay_all, weight_all, long_all, short_chan, taps_own,
     )
 
     rim_after = from_behind(heads, AXES, -1)
@@ -400,16 +552,30 @@
     gq, gk, gv = pl.pallas_call(
         functools.partial(edge_kernel, cpg, width, tap_count),
         grid=(steps,),
-        in_specs=[cols(3 * SUB), cols(3 * SUB), cols(3 * SUB, groups_own)] + [bottom] * 3,
+        in_specs=[cols(3 * SUB)] * 3 + [bottom] * 3,
         out_specs=[bottom] * 3,
         out_shape=[big] * 3,
         input_output_aliases={3: 0, 4: 1, 5: 2},
         compiler_params=params(),
         name="edge",
-    )(rim_after, tails, short_all, gq, gk, gv)
-
-    owned = lax.psum_scatter(taps_part, "own", scatter_dimension=1, tiled=True)
-    grad_taps = lax.psum(owned, "ctx").astype(f32)
+    )(rim_after, tails, short_chan, gq, gk, gv)
+
+    ctxs = count // owners
+    high = rows // ctxs
+    shares = taps_part.reshape(ctxs, high, owners, groups_own).transpose(0, 2, 1, 3)
+    grad_taps = pl.pallas_call(
+        functools.partial(reduce_kernel, owners, count),
+        in_specs=[vmem],
+        out_specs=vmem,
+        out_shape=shape((ctxs, high, groups_own), f32),
+        scratch_shapes=[
+            pltpu.VMEM((count, high, groups_own), f32),
+            pltpu.SemaphoreType.DMA((count,)), pltpu.SemaphoreType.DMA((count,)),
+            pltpu.SemaphoreType.DMA((ctxs,)), pltpu.SemaphoreType.DMA((ctxs,)),
+        ],
+        compiler_params=remote(2),
+        name="reduce",
+    )(shares.reshape(count, high, groups_own)).reshape(rows, groups_own)
     return (layer_out, gq, gk, gv, grad_taps)
 
 

time: 278 us -> 207 us (0.74)
  Pallas kernels: 99.1 us -> 178 us
  blocking collectives: 59 us -> 0 us
  waiting for transfers between devices: 48.7 us -> 0.01 us
  starting transfers between devices: 36.1 us -> 7.95 us
  between operations: 14.2 us -> 0.89 us
  other arithmetic: 6.28 us -> 2.17 us
  local copies, waits for them, and re-layouts: 13.8 us -> 16.9 us
    pallas_call x1 -> x3, Pallas kernels: 2.06 us -> 88 us  [the longest x1 57.5 us: shards(): pl.pallas_call(functools.partial(exchange_kernel, owners, count), in_spec...]
    psum x1 -> x0, blocking collectives: 37.1 us -> none  [shards(): grad_taps = lax.psum(owned, 'ctx').astype(f32)]
    all_to_all x2 -> x0, starting transfers between devices: 28.7 us -> none  [the longest x1 18.8 us: shards(): returned = lax.all_to_all(scanned.astype(bf16), AXES, 0, 0, tiled=True)]
    all_to_all x2 -> x0, waiting for transfers between devices: 27.2 us -> none  [the longest x1 27.2 us: shards(): got = lax.all_to_all(sent, AXES, 0, 0, tiled=True).astype(f32)]
    all_gather x3 -> x0, blocking collectives: 21.9 us -> none  [the longest x1 9.55 us: shards(): lax.all_gather(jnp.concatenate([decay_rate, weight_own], axis=0), 'own',...]
    unnamed x2 -> x0, waiting for transfers between devices: 21.5 us -> none
    pallas_call x1, Pallas kernels: 8.87 us -> 3.74 us  [shards(): pl.pallas_call(functools.partial(edge_kernel, cpg, width, tap_count), gri...]
    convert_element_type x3 -> x1, other arithmetic: 3.26 us -> 0.01 us  [shards(): long_taps.astype(bf16)]
  transfers between devices with their start and end apart: 7 -> 4, of which waited for: 2 -> 0; matrix products, arithmetic and copies ran while one was open for 4% -> 3% of each run, Pallas kernels for 9% -> 54%
where the time goes in v2:
time: 207 us; the launch traced here: 206 us
  Pallas kernels  178 us (86%)
  local copies, waits for them, and re-layouts  16.9 us (8%)
  starting transfers between devices  7.95 us (4%)
  other arithmetic  2.17 us (1%)
    pallas_call x1, Pallas kernels, shards(): pl.pallas_call(functools.partial(exchange_kernel, owners, count), in_spec...  57.5 us
    pallas_call x1, Pallas kernels, shards(): pl.pallas_call(functools.partial(last_kernel, cpg, width, tap_count, scal...  36.2 us
    pallas_call x1, Pallas kernels, shards(): pl.pallas_call(functools.partial(first_kernel, cpg, width, tap_count), gr...  27.8 us
    pallas_call x1, Pallas kernels, shards(): pl.pallas_call(functools.partial(reduce_kernel, owners, count), in_specs=...  22.3 us
    pallas_call x1, Pallas kernels, shards(): pl.pallas_call(functools.partial(own_kernel, cpg, width), grid=(steps,),...  22.1 us
    unnamed x23, local copies, waits for them, and re-layouts  10.3 us
    pallas_call x1, Pallas kernels, shards(): pl.pallas_call(functools.partial(gather_kernel, owners), in_specs=[vmem]...  8.28 us
    ppermute x4, starting transfers between devices, from_behind(): lax.ppermute(value, axis, [(source, source + steps) for source in range(l...  7.95 us
  transfers between devices with their start and end apart: 4, of which 0 were waited for; matrix products, arithmetic and copies ran while one was open for 3% of the time, Pallas kernels for 54%

profile of v2, /device:TPU:0, one launch (start us, length us, event | category | flops | bytes accessed | tf_op | source)
XLA Modules:
  0.0 205.8 jit_solution(4024322558236165078)
XLA Ops:
  0.6 0.9 slice.9
  1.5 0.9 slice.10
  2.5 0.9 slice.11
  3.4 2.4 %collective-permute-start = (bf16[24,8192]{1,0:T(8,128)(2,1)S(1)}, bf16[24,8192]{1,0:T(8,128)(2,1)S(1)}, u32[]{:S(2)}, u32[]{:S(2)}) collective-permute-start(bf16[24,8192]{1,0:T(8,128)(2,1)S(1)} %pad_maximum_fusion), channel_id=1, source_target_pairs={{0,1},{1,2},{2,3},{3,4},{4,5},{5,6},{6,7},{7,8},{8,9},{9,10},{10,1... | collective-permute-start | bytes 1179656 | tf_op jit(solution)/shard_map/ppermute | solution.py:20
  5.8 0.7 pad_bitcast_fusion.first_ref
  6.5 0.8 copy-done.6
  7.4 8.3 %gather.1 = (f32[4,24,128]{2,1,0:T(8,128)S(1)}, f32[4,8,2048]{2,1,0:T(8,128)S(1)}) custom-call(f32[24,128]{1,0:T(8,128)S(1)} %pad_bitcast_fusion.first_ref, f32[8,2048]{1,0:T(8,128)S(1)} %copy-done.6), custom_call_target="tpu_custom_call" | custom-call | tf_op jit(solution)/shard_map/gather/pallas_call | solution.py:437
  15.7 27.8 %first.1 = (bf16[128,8192]{1,0:T(8,128)(2,1)S(1)}, bf16[128,8192]{1,0:T(8,128)(2,1)S(1)}, bf16[128,8192]{1,0:T(8,128)(2,1)}, bf16[128,8192]{1,0:T(8,128)(2,1)}, ...) custom-call(bf16[128,8192]{1,0:T(8,128)(2,1)} %q_ref.1, bf16[128,8192]{1,0:T(8,128)(2,1)} %k_ref.1, ...), custom_call_target="tpu_custom_call" | custom-call | flops 104857600 | bytes 18874368 | tf_op jit(solution)/shard_map/first/pallas_call | solution.py:460
  43.5 1.3 copy-done
  44.8 1.3 copy-done.1
  46.2 0.7 copy-done.8
  46.9 3.0 %collective-permute-start.1 = (bf16[128,8192]{1,0:T(8,128)(2,1)}, bf16[128,8192]{1,0:T(8,128)(2,1)S(1)}, u32[]{:S(2)}, u32[]{:S(2)}) collective-permute-start(bf16[128,8192]{1,0:T(8,128)(2,1)} %get-tuple-element.32.p_ref), channel_id=1, source_target_pairs={{0,1},{1,2},{2,3},{3,4},{4,5},{5,6},{6,7},{7,8},{8,9},{9,10},{10,1... | collective-permute-start | bytes 6291464 | tf_op jit(solution)/shard_map/ppermute | solution.py:20
  49.9 1.3 collective-permute-start.2
  51.2 0.6 cosine_convert_fusion
  51.8 0.6 fusion
  52.4 0.1 copy.24.here_ref
  52.6 1.0 copy.25.before_ref
  53.6 0.9 sqrt_multiply_fusion.w_ref
  54.5 1.0 copy.30
  55.4 57.5 %exchange.1 = (bf16[32,16,256]{2,1,0:T(8,128)(2,1)S(1)}, f32[4,8,2048]{2,1,0:T(8,128)S(1)}, bf16[4,128,128]{2,1,0:T(8,128)(2,1)S(1)}) custom-call(bf16[32,16,256]{2,1,0:T(8,128)(2,1)S(1)} %bitcast.22, f32[8,256]{1,0:T(8,128)S(1)} %multiply_bitcast_fusion.rate_ref, f32[8,2048]{1,0:T(8,128)S(1)} %sqrt_multiply_fusion.w_ref, ...), custom_call_target="tpu_custom_call" | custom-call | tf_op jit(solution)/shard_map/exchange/pallas_call | solution.py:485
  113.0 22.1 %own.1 = (bf16[128,8192]{1,0:T(8,128)(2,1)S(1)}, bf16[128,8192]{1,0:T(8,128)(2,1)S(1)}, f32[128,512]{1,0:T(8,128)S(1)}) custom-call(bf16[256,128]{1,0:T(8,128)(2,1)S(1)} %copy.24.here_ref, bf16[128,256]{1,0:T(8,128)(2,1)S(1)} %fusion.7.back_ref, bf16[128,8192]{1,0:T(8,128)(2,1)} %get-tuple-element.32.p_ref, bf16[128,8192]{1,0:T(8,128)(2,1)} %get-tuple-element.33.gc_ref, ...), custom_call_target="tpu_custom_call" | custom-call | flops 1879048192 | bytes 8388608 | tf_op jit(solution)/shard_map/own/pallas_call | solution.py:504
  135.1 1.4 copy-done.2
  136.5 1.4 copy-done.3
  137.9 36.2 %last.1 = (bf16[128,8192]{1,0:T(8,128)(2,1)}, bf16[128,8192]{1,0:T(8,128)(2,1)}, bf16[128,8192]{1,0:T(8,128)(2,1)}, bf16[128,8192]{1,0:T(8,128)(2,1)}, bf16[24,8...) custom-call(bf16[256,128]{1,0:T(8,128)(2,1)S(1)} %copy.24.here_ref, ...), custom_call_target="tpu_custom_call" | custom-call | flops 2147483648 | bytes 27262976 | tf_op jit(solution)/shard_map/last/pallas_call | solution.py:522
  174.1 0.9 copy-done.4
  175.0 0.7 copy-done.9
  175.7 1.3 collective-permute-start.3
  177.0 1.0 reshape.45
  178.0 22.3 %reduce.1 = f32[8,16,128]{2,1,0:T(8,128)S(1)} custom-call(f32[32,16,128]{2,1,0:T(8,128)S(1)} %bitcast.21), custom_call_target="tpu_custom_call" | custom-call | tf_op jit(solution)/shard_map/reduce/pallas_call | solution.py:566
  200.3 1.1 copy-done.5
  201.4 3.7 %edge.1 = (bf16[128,8192]{1,0:T(8,128)(2,1)}, bf16[128,8192]{1,0:T(8,128)(2,1)}, bf16[128,8192]{1,0:T(8,128)(2,1)}) custom-call(bf16[24,8192]{1,0:T(8,128)(2,1)S(1)} %collective-permute-done.3.rim_ref, f32[24,8192]{1,0:T(8,128)S(1)} %copy-done.5, ...), custom_call_target="tpu_custom_call", output_to_operand_aliasing={{0}: (3, {}), {1}: (4, {}), {2}: (5, {})} | custom-call | tf_op jit(solution)/shard_map/edge/pallas_call | solution.py:552
  205.2 0.6 copy.35
  (25 shorter events, 0.1 us)
Async XLA Ops:
  3.4 12.2 %collective-permute-start = (bf16[24,8192]{1,0:T(8,128)(2,1)S(1)}, bf16[24,8192]{1,0:T(8,128)(2,1)S(1)}, u32[]{:S(2)}, u32[]{:S(2)}) collective-permute-start(bf16[24,8192]{1,0:T(8,128)(2,1)S(1)} %pad_maximum_fusion), channel_id=1, source_target_pairs={{0,1},{1,2},{2,3},{3,4},{4,5},{5,6},{6,7},{7,8},{8,9},{9,10},{10,1... | collective-permute-start | bytes 1179656 | tf_op jit(solution)/shard_map/ppermute | solution.py:20
  6.5 0.8 copy-start.6
  15.7 35.5 %copy-start.10 = (f32[128,128]{1,0:T(8,128)S(1)}, f32[128,128]{1,0:T(8,128)}, u32[]{:S(2)}) copy-start(f32[128,128]{1,0:T(8,128)} %param.12) | copy-start | bytes 196612
  15.7 37.9 %copy-start.7 = (f32[8,2048]{1,0:T(8,128)S(1)}, f32[8,2048]{1,0:T(8,128)}, u32[]{:S(2)}) copy-start(f32[8,2048]{1,0:T(8,128)} %second_ref.1) | copy-start | bytes 196612
  43.5 1.3 copy-start
  44.8 1.3 copy-start.1
  46.2 0.7 copy-start.8
  46.9 91.0 %collective-permute-start.1 = (bf16[128,8192]{1,0:T(8,128)(2,1)}, bf16[128,8192]{1,0:T(8,128)(2,1)S(1)}, u32[]{:S(2)}, u32[]{:S(2)}) collective-permute-start(bf16[128,8192]{1,0:T(8,128)(2,1)} %get-tuple-element.32.p_ref), channel_id=1, source_target_pairs={{0,1},{1,2},{2,3},{3,4},{4,5},{5,6},{6,7},{7,8},{8,9},{9,10},{10,1... | collective-permute-start | bytes 6291464 | tf_op jit(solution)/shard_map/ppermute | solution.py:20
  49.9 88.0 %collective-permute-start.2 = (bf16[128,8192]{1,0:T(8,128)(2,1)}, bf16[128,8192]{1,0:T(8,128)(2,1)}, u32[]{:S(2)}, u32[]{:S(2)}) collective-permute-start(bf16[128,8192]{1,0:T(8,128)(2,1)} %get-tuple-element.33.gc_ref), channel_id=1, source_target_pairs={{1,0},{2,1},{3,2},{4,3},{5,4},{6,5},{7,6},{8,7},{9,8},{10,9},{11,1... | collective-permute-start | bytes 6291464 | tf_op jit(solution)/shard_map/ppermute | solution.py:20
  135.1 1.4 copy-start.2
  136.5 1.4 copy-start.3
  174.1 0.9 copy-start.4
  175.0 0.7 copy-start.9
  175.7 24.6 %collective-permute-start.3 = (bf16[24,8192]{1,0:T(8,128)(2,1)}, bf16[24,8192]{1,0:T(8,128)(2,1)S(1)}, u32[]{:S(2)}, u32[]{:S(2)}) collective-permute-start(bf16[24,8192]{1,0:T(8,128)(2,1)} %get-tuple-element.46), channel_id=1, source_target_pairs={{1,0},{2,1},{3,2},{4,3},{5,4},{6,5},{7,6},{8,7},{9,8},{10,9},{11,1... | collective-permute-start | bytes 1179656 | tf_op jit(solution)/shard_map/ppermute | solution.py:20
  200.3 1.1 copy-start.5

commit v3 on v2

--- a/solution.py
+++ b/solution.py
@@ -10,6 +10,7 @@
 
 AXES = ("ctx", "own")
 SUB = 8
+LAST_INPUTS = 18
 f32, bf16 = jnp.float32, jnp.bfloat16
 VMEM_LIMIT = 48 * 1024 * 1024
 
@@ -154,7 +155,10 @@
     pl.semaphore_wait(barrier, count - 1)
 
 
-def gather_kernel(owners, first_ref, second_ref, first_out, second_out, send, recv):
+def gather_kernel(owners, *refs):
+    number = (len(refs) - 2) // 2
+    pairs = list(zip(refs[:number], refs[number : 2 * number]))
+    send, recv = refs[2 * number :]
     ctx, own = lax.axis_index("ctx"), lax.axis_index("own")
 
     def device(k):
@@ -165,18 +169,17 @@
     def copies(k):
         return [
             put(src, dst.at[own], send.at[n, k], recv.at[n, k], device(k))
-            for n, (src, dst) in enumerate(((first_ref, first_out), (second_ref, second_out)))
+            for n, (src, dst) in enumerate(pairs)
         ]
 
     loop(owners, lambda k: [c.start() for c in copies(k)] and None)
-    first_out[own] = first_ref[...]
-    second_out[own] = second_ref[...]
+    for src, dst in pairs:
+        dst[own] = src[...]
     loop(owners, lambda k: [c.wait() for c in copies(k)] and None)
 
 
 def exchange_kernel(
-    owners, count, st_ref, rate_ref, w_ref, l_ref, ret_ref, w_out, l_out,
-    got, work, scanned, send, recv, gsend, grecv,
+    owners, count, st_ref, rate_ref, ret_ref, got, work, scanned, send, recv,
 ):
     ctx, own = lax.axis_index("ctx"), lax.axis_index("own")
     me = ctx * owners + own
@@ -195,18 +198,8 @@
         to = lax.rem(me + k, count)
         return put(scanned.at[to], ret_ref.at[me], send.at[1, k], recv.at[1, k], device(k))
 
-    def gathers(k):
-        peer = (ctx, lax.rem(own + k, owners))
-        return [
-            put(src, dst.at[own], gsend.at[n, k], grecv.at[n, k], peer)
-            for n, (src, dst) in enumerate(((w_ref, w_out), (l_ref, l_out)))
-        ]
-
     loop(count, lambda k: out_copy(k).start())
-    loop(owners, lambda k: [c.start() for c in gathers(k)] and None)
     got[me] = st_ref[me]
-    w_out[own] = w_ref[...]
-    l_out[own] = l_ref[...]
     loop(count, lambda k: out_copy(k).wait())
     keep = jnp.exp(-rate_ref[...])
 
@@ -226,7 +219,6 @@
     loop(count, lambda k: back_copy(k).start())
     ret_ref[me] = scanned[me]
     loop(count, lambda k: back_copy(k).wait())
-    loop(owners, lambda k: [c.wait() for c in gathers(k)] and None)
 
 
 def reduce_kernel(owners, count, part_ref, out_ref, got, send, recv, asend, arecv):
@@ -384,6 +376,10 @@
     taps_ref[...] = total * scale
 
 
+def last_again(cpg, width, taps, scale, *refs):
+    last_kernel(cpg, width, taps, scale, *refs[:LAST_INPUTS], *refs[LAST_INPUTS + 4 :])
+
+
 def edge_kernel(cpg, width, taps, rim_ref, tail_ref, short_ref, *refs):
     olds, outs = refs[:3], refs[3:]
 
@@ -434,118 +430,149 @@
         3 * SUB, groups_own
     )
     weight_own = residues * jnp.sqrt(-jnp.expm1(-2.0 * decay_rate))
-    short_all, decay_all = pl.pallas_call(
+    mine = (short_pad, decay_rate, weight_own, long_taps.astype(bf16))
+    short_all, decay_all, weight_all, long_all = pl.pallas_call(
         functools.partial(gather_kernel, owners),
-        in_specs=[vmem] * 2,
-        out_specs=[vmem] * 2,
-        out_shape=[
-            shape((owners,) + short_pad.shape, f32), shape((owners,) + decay_rate.shape, f32)
-        ],
-        scratch_shapes=[pltpu.SemaphoreType.DMA((2, owners))] * 2,
+        in_specs=[vmem] * 4,
+        out_specs=[vmem] * 4,
+        out_shape=[shape((owners,) + x.shape, x.dtype) for x in mine],
+        scratch_shapes=[pltpu.SemaphoreType.DMA((4, owners))] * 2,
         compiler_params=remote(0),
         name="gather",
-    )(short_pad, decay_rate)
+    )(*mine)
     here, before, back = odd_tables(rows)
+
+    cuts = 2 if steps % 2 == 0 else 1
+    piece = steps // cuts
+    part_chans = piece * tile
 
     def cols(height, wide=tile):
         return pl.BlockSpec((height, wide), lambda i: (0, i))
 
-    def owned(height, wide):
-        return pl.BlockSpec((None, height, wide), lambda i: (i, 0, 0))
+    def cut_cols(cut, height, wide=tile):
+        return pl.BlockSpec((height, wide), lambda i: (0, cut * piece + i))
+
+    def owned(cut, height, wide):
+        return pl.BlockSpec((None, height, wide), lambda i: (cut * piece + i, 0, 0))
 
     def whole(height, wide):
         return pl.BlockSpec((height, wide), lambda i: (0, 0))
 
     big = shape((rows, chans), bf16)
-    qf, kf, vf, product, conv, states, short_chan = pl.pallas_call(
-        functools.partial(first_kernel, cpg, width, tap_count),
-        grid=(steps,),
-        in_specs=[cols(rows)] * 4 + [cols(3 * SUB), owned(3 * SUB, groups_own), owned(poles, tile)],
-        out_specs=[cols(rows)] * 5 + [cols(2 * poles), cols(3 * SUB)],
-        out_shape=[big] * 5
-        + [shape((2 * poles, chans), bf16), shape((3 * SUB, chans), f32)],
-        compiler_params=params(),
-        cost_estimate=pl.CostEstimate(
-            flops=100 * rows * chans, bytes_accessed=18 * rows * chans, transcendentals=0
-        ),
-        name="first",
-    )(query_proj, key_proj, value_proj, grad_out, rims, short_all, decay_all)
-
-    earlier = from_behind(product, AXES, 1)
-    later = from_behind(conv, AXES, -1)
+    half = shape((rows, part_chans), bf16)
+    firsts, halos = [], []
+    for cut in range(cuts):
+        made = pl.pallas_call(
+            functools.partial(first_kernel, cpg, width, tap_count),
+            grid=(piece,),
+            in_specs=[cut_cols(cut, rows)] * 4
+            + [
+                cut_cols(cut, 3 * SUB), owned(cut, 3 * SUB, groups_own),
+                owned(cut, poles, tile),
+            ],
+            out_specs=[cols(rows)] * 5 + [cols(2 * poles), cols(3 * SUB)],
+            out_shape=[half] * 5
+            + [shape((2 * poles, part_chans), bf16), shape((3 * SUB, part_chans), f32)],
+            compiler_params=params(),
+            cost_estimate=pl.CostEstimate(
+                flops=6000 * rows * part_chans, bytes_accessed=18 * rows * part_chans,
+                transcendentals=0,
+            ),
+            name="first",
+        )(query_proj, key_proj, value_proj, grad_out, rims, short_all, decay_all)
+        firsts.append(made)
+        halos.append((from_behind(made[3], AXES, 1), from_behind(made[4], AXES, -1)))
+
+    nears = []
+    for cut in range(cuts):
+        nears.append(
+            pl.pallas_call(
+                functools.partial(own_kernel, cpg, width),
+                grid=(piece,),
+                in_specs=[
+                    whole(2 * rows, rows), whole(rows, 2 * rows), cols(rows), cols(rows),
+                    owned(cut, poles, tile), owned(cut, poles, tile),
+                    owned(cut, long_taps.shape[0], groups_own),
+                ],
+                out_specs=[cols(rows), cols(rows), cols(rows, groups_own)],
+                out_shape=[half, half, shape((rows, piece * groups_own), f32)],
+                scratch_shapes=[pltpu.VMEM((2 * rows, groups_own), f32)],
+                compiler_params=params(),
+                cost_estimate=pl.CostEstimate(
+                    flops=90 * rows * rows * part_chans,
+                    bytes_accessed=8 * rows * part_chans, transcendentals=0,
+                ),
+                name="own",
+            )(here, back, firsts[cut][3], firsts[cut][4], decay_all, weight_all, long_all)
+        )
 
     part = chans // count
+    states = jnp.concatenate([made[5] for made in firsts], axis=1)
+    short_chan = jnp.concatenate([made[6] for made in firsts], axis=1)
     sent = states.reshape(2 * poles, count, part).transpose(1, 0, 2)
     me = lax.axis_index("ctx") * owners + lax.axis_index("own")
     at_owner = lax.div(me * part, tile)
     rate = lax.dynamic_slice(
         decay_all, (at_owner, 0, me * part - at_owner * tile), (1, poles, part)
     )[0] * float(rows)
+    sent, nears = lax.optimization_barrier((sent, nears))
     slab = (count, 2 * poles, part)
-    returned, weight_all, long_all = pl.pallas_call(
+    returned = pl.pallas_call(
         functools.partial(exchange_kernel, owners, count),
-        in_specs=[vmem] * 4,
-        out_specs=[vmem] * 3,
-        out_shape=[
-            shape(slab, bf16),
-            shape((owners,) + weight_own.shape, f32),
-            shape((owners,) + long_taps.shape, bf16),
-        ],
+        in_specs=[vmem] * 2,
+        out_specs=vmem,
+        out_shape=shape(slab, bf16),
         scratch_shapes=[
             pltpu.VMEM(slab, bf16), pltpu.VMEM(slab, f32), pltpu.VMEM(slab, bf16),
             pltpu.SemaphoreType.DMA((2, count)), pltpu.SemaphoreType.DMA((2, count)),
-            pltpu.SemaphoreType.DMA((2, owners)), pltpu.SemaphoreType.DMA((2, owners)),
         ],
         compiler_params=remote(1),
         name="exchange",
-    )(sent, rate, weight_own, long_taps.astype(bf16))
+    )(sent, rate)
     state_in = returned.transpose(1, 0, 2).reshape(2 * poles, chans)
 
-    near, near_back, taps_own = pl.pallas_call(
-        functools.partial(own_kernel, cpg, width),
-        grid=(steps,),
-        in_specs=[
-            whole(2 * rows, rows), whole(rows, 2 * rows), cols(rows), cols(rows),
-            owned(poles, tile), owned(poles, tile), owned(long_taps.shape[0], groups_own),
-        ],
-        out_specs=[cols(rows), cols(rows), cols(rows, groups_own)],
-        out_shape=[big, big, shape((rows, groups), f32)],
-        scratch_shapes=[pltpu.VMEM((2 * rows, groups_own), f32)],
-        compiler_params=params(),
-        cost_estimate=pl.CostEstimate(
-            flops=14 * rows * rows * chans, bytes_accessed=8 * rows * chans, transcendentals=0
-        ),
-        name="own",
-    )(here, back, product, conv, decay_all, weight_all, long_all)
-
     scale = 1.0 / math.sqrt(rows * count * cpg)
-    layer_out, gq, gk, gv, heads, tails, taps_part = pl.pallas_call(
-        functools.partial(last_kernel, cpg, width, tap_count, scale),
-        grid=(steps,),
-        in_specs=[whole(2 * rows, rows), whole(2 * rows, rows), whole(rows, 2 * rows)]
-        + [cols(rows)] * 9
-        + [
-            cols(2 * poles), owned(poles, tile), owned(poles, tile),
-            owned(long_taps.shape[0], groups_own), cols(3 * SUB), cols(rows, groups_own),
-        ],
-        out_specs=[cols(rows)] * 4 + [cols(3 * SUB), cols(3 * SUB), cols(rows, groups_own)],
-        out_shape=[big] * 4
-        + [
-            shape((3 * SUB, chans), bf16), shape((3 * SUB, chans), f32),
-            shape((rows, groups), f32),
-        ],
-        scratch_shapes=[
-            pltpu.VMEM((2 * rows, groups_own), f32), pltpu.VMEM((2 * rows, groups_own), bf16)
-        ],
-        compiler_params=params(),
-        cost_estimate=pl.CostEstimate(
-            flops=16 * rows * rows * chans, bytes_accessed=26 * rows * chans, transcendentals=0
-        ),
-        name="last",
-    )(
-        here, before, back, earlier, later, conv, near, near_back, qf, kf, vf, grad_out,
-        state_in, decay_all, weight_all, long_all, short_chan, taps_own,
-    )
+    results, small = (), []
+    for cut in range(cuts):
+        qf, kf, vf, _, conv, _, short_part = firsts[cut]
+        near, near_back, taps_own = nears[cut]
+        outs = pl.pallas_call(
+            functools.partial(last_again if cut else last_kernel, cpg, width, tap_count, scale),
+            grid=(piece,),
+            in_specs=[whole(2 * rows, rows), whole(2 * rows, rows), whole(rows, 2 * rows)]
+            + [cols(rows)] * 8
+            + [
+                cut_cols(cut, rows), cut_cols(cut, 2 * poles), owned(cut, poles, tile),
+                owned(cut, poles, tile), owned(cut, long_taps.shape[0], groups_own),
+                cols(3 * SUB), cols(rows, groups_own),
+            ]
+            + [pl.BlockSpec(memory_space=pl.ANY)] * len(results),
+            out_specs=[cut_cols(cut, rows)] * 4
+            + [cols(3 * SUB), cols(3 * SUB), cols(rows, groups_own)],
+            out_shape=[big] * 4
+            + [
+                shape((3 * SUB, part_chans), bf16), shape((3 * SUB, part_chans), f32),
+                shape((rows, piece * groups_own), f32),
+            ],
+            input_output_aliases={LAST_INPUTS + n: n for n in range(len(results))},
+            scratch_shapes=[
+                pltpu.VMEM((2 * rows, groups_own), f32),
+                pltpu.VMEM((2 * rows, groups_own), bf16),
+            ],
+            compiler_params=params(),
+            cost_estimate=pl.CostEstimate(
+                flops=16 * rows * rows * part_chans, bytes_accessed=26 * rows * part_chans,
+                transcendentals=0,
+            ),
+            name="last",
+        )(
+            here, before, back, *halos[cut], conv, near, near_back, qf, kf, vf, grad_out,
+            state_in, decay_all, weight_all, long_all, short_part, taps_own, *results,
+        )
+        results = tuple(outs[:4])
+        small.append(outs[4:])
+    layer_out, gq, gk, gv = results
+    heads, tails, taps_part = (jnp.concatenate(x, axis=1) for x in zip(*small))
 
     rim_after = from_behind(heads, AXES, -1)
     bottom = pl.BlockSpec((2 * SUB, tile), lambda i: (rows // (2 * SUB) - 1, i))

time: 207 us -> 184 us (0.89)
  Pallas kernels: 178 us -> 153 us
  starting transfers between devices: 7.95 us -> 13.7 us
  local copies, waits for them, and re-layouts: 16.9 us -> 14 us
    pallas_call x1, Pallas kernels: 57.5 us -> 25 us  [shards(): pl.pallas_call(functools.partial(exchange_kernel, owners, count), in_spec...]
    ppermute x4 -> x6, starting transfers between devices: 7.95 us -> 13.7 us  [from_behind(): lax.ppermute(value, axis, [(source, source + steps) for source in range(l...]
    pallas_call x1, Pallas kernels: 8.28 us -> 12.7 us  [shards(): pl.pallas_call(functools.partial(gather_kernel, owners), in_specs=[vmem]...]
    pallas_call x2 -> x4, Pallas kernels: 58.3 us -> 61.1 us  [the longest x2 39 us: shards(): pl.pallas_call(functools.partial(last_again if cut else last_kernel, cpg,...]
    pallas_call x1 -> x2, Pallas kernels: 27.8 us -> 30 us  [shards(): pl.pallas_call(functools.partial(first_kernel, cpg, width, tap_count), gr...]
    unnamed x23 -> x33, local copies, waits for them, and re-layouts: 10.3 us -> 10.8 us
  transfers between devices with their start and end apart: 4 -> 6, of which waited for: 0 -> 0; matrix products, arithmetic and copies ran while one was open for 3% -> 1% of each run, Pallas kernels for 54% -> 63%
where the time goes in v3:
time: 184 us
  Pallas kernels  153 us (83%)
  local copies, waits for them, and re-layouts  14 us (8%)
  starting transfers between devices  13.7 us (7%)
    pallas_call x2, Pallas kernels, shards(): pl.pallas_call(functools.partial(last_again if cut else last_kernel, cpg,...  39 us
    pallas_call x2, Pallas kernels, shards(): pl.pallas_call(functools.partial(first_kernel, cpg, width, tap_count), gr...  30 us
    pallas_call x1, Pallas kernels, shards(): pl.pallas_call(functools.partial(exchange_kernel, owners, count), in_spec...  25 us
    pallas_call x2, Pallas kernels, shards(): pl.pallas_call(functools.partial(own_kernel, cpg, width), grid=(piece,),...  22.1 us
    pallas_call x1, Pallas kernels, shards(): pl.pallas_call(functools.partial(reduce_kernel, owners, count), in_specs=...  20.5 us
    ppermute x6, starting transfers between devices, from_behind(): lax.ppermute(value, axis, [(source, source + steps) for source in range(l...  13.7 us
    pallas_call x1, Pallas kernels, shards(): pl.pallas_call(functools.partial(gather_kernel, owners), in_specs=[vmem]...  12.7 us
    unnamed x33, local copies, waits for them, and re-layouts  10.8 us
  transfers between devices with their start and end apart: 6, of which 0 were waited for; matrix products, arithmetic and copies ran while one was open for 1% of the time, Pallas kernels for 63%

profile of v3, /device:TPU:0, one launch (start us, length us, event | category | flops | bytes accessed | tf_op | source)
XLA Modules:
  0.0 183.6 jit_solution(12878889948005890132)
XLA Ops:
  0.7 1.0 slice.10
  1.6 0.9 slice.11
  2.6 0.9 slice.9
  3.5 2.4 %collective-permute-start = (bf16[24,8192]{1,0:T(8,128)(2,1)S(1)}, bf16[24,8192]{1,0:T(8,128)(2,1)S(1)}, u32[]{:S(2)}, u32[]{:S(2)}) collective-permute-start(bf16[24,8192]{1,0:T(8,128)(2,1)S(1)} %pad_maximum_fusion.2), channel_id=1, source_target_pairs={{0,1},{1,2},{2,3},{3,4},{4,5},{5,6},{6,7},{7,8},{8,9},{9,10},{10,1... | collective-permute-start | bytes 1179656 | tf_op jit(solution)/shard_map/ppermute | solution.py:21
  5.9 0.9 sqrt_multiply_fusion.refs_2_
  6.8 0.6 cosine_convert_fusion
  7.8 12.7 %gather.1 = (f32[4,24,128]{2,1,0:T(8,128)S(1)}, f32[4,8,2048]{2,1,0:T(8,128)S(1)}, f32[4,8,2048]{2,1,0:T(8,128)S(1)}, bf16[4,128,128]{2,1,0:T(8,128)(2,1)S(1)}) custom-call(f32[24,128]{1,0:T(8,128)S(1)} %pad_bitcast_fusion.refs_0_, f32[8,2048]{1,0:T(8,128)S(1)} %copy-done.13, f32[8,2048]{1,0:T(8,128)S(1)} %sqrt_multiply_fusion.refs_2_, ...), custom_call_target="tpu_custom_call" | custom-call | tf_op jit(solution)/shard_map/gather/pallas_call | solution.py:434
  20.5 15.1 %first.3 = (bf16[128,4096]{1,0:T(8,128)(2,1)S(1)}, bf16[128,4096]{1,0:T(8,128)(2,1)S(1)}, bf16[128,4096]{1,0:T(8,128)(2,1)S(1)}, bf16[128,4096]{1,0:T(8,128)(2,1...) custom-call(bf16[128,8192]{1,0:T(8,128)(2,1)} %q_ref.3, ...), custom_call_target="tpu_custom_call" | custom-call | flops 3145728000 | bytes 9437184 | tf_op jit(solution)/shard_map/first/pallas_call | solution.py:465
  35.6 1.0 copy-done.7
  36.5 1.1 copy-done.8
  37.6 1.0 copy-done.9
  38.6 1.3 collective-permute-start.4
  39.9 3.2 %collective-permute-start.3 = (bf16[128,4096]{1,0:T(8,128)(2,1)}, bf16[128,4096]{1,0:T(8,128)(2,1)S(1)}, u32[]{:S(2)}, u32[]{:S(2)}) collective-permute-start(bf16[128,4096]{1,0:T(8,128)(2,1)} %get-tuple-element.59.p_ref), channel_id=1, source_target_pairs={{0,1},{1,2},{2,3},{3,4},{4,5},{5,6},{6,7},{7,8},{8,9},{9,10},{10,1... | collective-permute-start | bytes 3145736 | tf_op jit(solution)/shard_map/ppermute | solution.py:21
  43.1 15.0 %first.2 = (bf16[128,4096]{1,0:T(8,128)(2,1)S(1)}, bf16[128,4096]{1,0:T(8,128)(2,1)S(1)}, bf16[128,4096]{1,0:T(8,128)(2,1)S(1)}, bf16[128,4096]{1,0:T(8,128)(2,1...) custom-call(bf16[128,8192]{1,0:T(8,128)(2,1)} %q_ref.3, ...), custom_call_target="tpu_custom_call" | custom-call | flops 3145728000 | bytes 9437184 | tf_op jit(solution)/shard_map/first/pallas_call | solution.py:465
  58.1 1.0 copy-done
  59.1 1.0 copy-done.1
  60.1 1.0 copy-done.2
  61.1 1.3 collective-permute-start.2
  62.4 4.3 %collective-permute-start.1 = (bf16[128,4096]{1,0:T(8,128)(2,1)S(1)}, bf16[128,4096]{1,0:T(8,128)(2,1)S(1)}, u32[]{:S(2)}, u32[]{:S(2)}) collective-permute-start(bf16[128,4096]{1,0:T(8,128)(2,1)S(1)} %get-tuple-element.55.p_ref), channel_id=1, source_target_pairs={{0,1},{1,2},{2,3},{3,4},{4,5},{5,6},{6,7},{7,8},{8,9},{9,10},{10,1... | collective-permute-start | bytes 3145736 | tf_op jit(solution)/shard_map/ppermute | solution.py:21
  66.7 1.2 copy-done.3
  67.9 10.6 %own.3 = (bf16[128,4096]{1,0:T(8,128)(2,1)S(1)}, bf16[128,4096]{1,0:T(8,128)(2,1)S(1)}, f32[128,256]{1,0:T(8,128)S(1)}) custom-call(bf16[256,128]{1,0:T(8,128)(2,1)S(1)} %copy.34.here_ref.refs_0_, bf16[128,256]{1,0:T(8,128)(2,1)S(1)} %fusion.7.back_ref.refs_2_, bf16[128,4096]{1,0:T(8,128)(2,1)S(1)} %get-tuple-element.55.p_ref, ...), custom_call_target="tpu_custom_call" | custom-call | flops 6039797760 | bytes 4194304 | tf_op jit(solution)/shard_map/own/pallas_call | solution.py:489
  78.5 1.0 copy-done.5
  79.5 1.0 copy-done.6
  80.5 11.5 %own.2 = (bf16[128,4096]{1,0:T(8,128)(2,1)S(1)}, bf16[128,4096]{1,0:T(8,128)(2,1)S(1)}, f32[128,256]{1,0:T(8,128)S(1)}) custom-call(bf16[256,128]{1,0:T(8,128)(2,1)S(1)} %copy.34.here_ref.refs_0_, bf16[128,256]{1,0:T(8,128)(2,1)S(1)} %fusion.7.back_ref.refs_2_, bf16[128,4096]{1,0:T(8,128)(2,1)} %get-tuple-element.59.p_ref, bf16[128,4096]{1,0:T(8,128)(2,1)S(1)} %copy-done.10, ...), custom_call_target="tpu_custom_call" | custom-call | flops 6039797760 | bytes 4194304 | tf_op jit(solution)/shard_map/own/pallas_call | solution.py:489
  92.0 1.0 copy-done.12
  93.0 25.0 %exchange.1 = bf16[32,16,256]{2,1,0:T(8,128)(2,1)S(1)} custom-call(bf16[32,16,256]{2,1,0:T(8,128)(2,1)S(1)} %bitcast.23, f32[8,256]{1,0:T(8,128)S(1)} %multiply_bitcast_fusion.rate_ref), custom_call_target="tpu_custom_call" | custom-call | tf_op jit(solution)/shard_map/exchange/pallas_call | solution.py:520
  118.2 19.5 %last.2 = (bf16[128,8192]{1,0:T(8,128)(2,1)}, bf16[128,8192]{1,0:T(8,128)(2,1)}, bf16[128,8192]{1,0:T(8,128)(2,1)}, bf16[128,8192]{1,0:T(8,128)(2,1)}, bf16[24,4...) custom-call(bf16[256,128]{1,0:T(8,128)(2,1)S(1)} %copy.34.here_ref.refs_0_, ...), custom_call_target="tpu_custom_call" | custom-call | flops 1073741824 | bytes 13631488 | tf_op jit(solution)/shard_map/last/pallas_call | solution.py:539
  137.7 19.5 %last.3 = (bf16[128,8192]{1,0:T(8,128)(2,1)}, bf16[128,8192]{1,0:T(8,128)(2,1)}, bf16[128,8192]{1,0:T(8,128)(2,1)}, bf16[128,8192]{1,0:T(8,128)(2,1)}, bf16[24,4...) custom-call(bf16[256,128]{1,0:T(8,128)(2,1)S(1)} %copy.34.here_ref.r, ...), custom_call_target="tpu_custom_call", output_to_operand_aliasing={{0}: (18, {}), {1}: (19, {}), {2}: (20, {}), {3}: (21, {})} | custom-call | flops 1073741824 | bytes 13631488 | tf_op jit(solution)/shard_map/last/pallas_call | solution.py:539
  157.2 1.3 collective-permute-start.5
  158.7 20.5 %reduce.1 = f32[8,16,128]{2,1,0:T(8,128)S(1)} custom-call(f32[32,16,128]{2,1,0:T(8,128)S(1)} %bitcast.22), custom_call_target="tpu_custom_call" | custom-call | tf_op jit(solution)/shard_map/reduce/pallas_call | solution.py:593
  179.2 3.8 %edge.1 = (bf16[128,8192]{1,0:T(8,128)(2,1)}, bf16[128,8192]{1,0:T(8,128)(2,1)}, bf16[128,8192]{1,0:T(8,128)(2,1)}) custom-call(bf16[24,8192]{1,0:T(8,128)(2,1)S(1)} %collective-permute-done.5.rim_ref, f32[24,8192]{1,0:T(8,128)S(1)} %pad_maximum_fusion.tail_ref, ...), custom_call_target="tpu_custom_call", output_to_operand_aliasing={{0}: (3, {}), {1}: (4, {}), {2}: (5, {})} | custom-call | tf_op jit(solution)/shard_map/edge/pallas_call | solution.py:579
  183.0 0.6 copy.49
  (47 shorter events, 0.7 us)
Async XLA Ops:
  0.6 7.1 %copy-start.13 = (f32[8,2048]{1,0:T(8,128)S(1)}, f32[8,2048]{1,0:T(8,128)}, u32[]{:S(2)}) copy-start(f32[8,2048]{1,0:T(8,128)} %refs_1_.1) | copy-start | bytes 196612
  0.6 6.8 %copy-start.14 = (f32[128,128]{1,0:T(8,128)S(1)}, f32[128,128]{1,0:T(8,128)}, u32[]{:S(2)}) copy-start(f32[128,128]{1,0:T(8,128)} %param.12) | copy-start | bytes 196612
  0.7 7.1 %copy-start.15 = (f32[3,7,128]{2,1,0:T(8,128)S(1)}, f32[3,7,128]{2,1,0:T(8,128)}, u32[]{:S(2)}) copy-start(f32[3,7,128]{2,1,0:T(8,128)} %param.11) | copy-start | bytes 32260
  3.5 17.0 %collective-permute-start = (bf16[24,8192]{1,0:T(8,128)(2,1)S(1)}, bf16[24,8192]{1,0:T(8,128)(2,1)S(1)}, u32[]{:S(2)}, u32[]{:S(2)}) collective-permute-start(bf16[24,8192]{1,0:T(8,128)(2,1)S(1)} %pad_maximum_fusion.2), channel_id=1, source_target_pairs={{0,1},{1,2},{2,3},{3,4},{4,5},{5,6},{6,7},{7,8},{8,9},{9,10},{10,1... | collective-permute-start | bytes 1179656 | tf_op jit(solution)/shard_map/ppermute | solution.py:21
  35.5 1.0 copy-start.7
  36.5 1.1 copy-start.8
  37.6 1.0 copy-start.9
  38.6 79.5 %collective-permute-start.4 = (bf16[128,4096]{1,0:T(8,128)(2,1)}, bf16[128,4096]{1,0:T(8,128)(2,1)S(1)}, u32[]{:S(2)}, u32[]{:S(2)}) collective-permute-start(bf16[128,4096]{1,0:T(8,128)(2,1)} %get-tuple-element.60.gc_ref), channel_id=1, source_target_pairs={{1,0},{2,1},{3,2},{4,3},{5,4},{6,5},{7,6},{8,7},{9,8},{10,9},{11,1... | collective-permute-start | bytes 3145736 | tf_op jit(solution)/shard_map/ppermute | solution.py:21
  39.9 78.2 %collective-permute-start.3 = (bf16[128,4096]{1,0:T(8,128)(2,1)}, bf16[128,4096]{1,0:T(8,128)(2,1)S(1)}, u32[]{:S(2)}, u32[]{:S(2)}) collective-permute-start(bf16[128,4096]{1,0:T(8,128)(2,1)} %get-tuple-element.59.p_ref), channel_id=1, source_target_pairs={{0,1},{1,2},{2,3},{3,4},{4,5},{5,6},{6,7},{7,8},{8,9},{9,10},{10,1... | collective-permute-start | bytes 3145736 | tf_op jit(solution)/shard_map/ppermute | solution.py:21
  58.1 1.0 copy-start
  59.1 1.0 copy-start.1
  60.1 1.0 copy-start.2
  61.1 76.6 %collective-permute-start.2 = (bf16[128,4096]{1,0:T(8,128)(2,1)}, bf16[128,4096]{1,0:T(8,128)(2,1)S(1)}, u32[]{:S(2)}, u32[]{:S(2)}) collective-permute-start(bf16[128,4096]{1,0:T(8,128)(2,1)} %get-tuple-element.56.gc_ref.refs_5_), channel_id=1, source_target_pairs={{1,0},{2,1},{3,2},{4,3},{5,4},{6,5},{7,6},{8,7},{9,8},{10,9},{11,1... | collective-permute-start | bytes 3145736 | tf_op jit(solution)/shard_map/ppermute | solution.py:21
  62.4 75.3 %collective-permute-start.1 = (bf16[128,4096]{1,0:T(8,128)(2,1)S(1)}, bf16[128,4096]{1,0:T(8,128)(2,1)S(1)}, u32[]{:S(2)}, u32[]{:S(2)}) collective-permute-start(bf16[128,4096]{1,0:T(8,128)(2,1)S(1)} %get-tuple-element.55.p_ref), channel_id=1, source_target_pairs={{0,1},{1,2},{2,3},{3,4},{4,5},{5,6},{6,7},{7,8},{8,9},{9,10},{10,1... | collective-permute-start | bytes 3145736 | tf_op jit(solution)/shard_map/ppermute | solution.py:21
  66.7 1.2 copy-start.3
  67.9 12.6 %copy-start.10 = (bf16[128,4096]{1,0:T(8,128)(2,1)S(1)}, bf16[128,4096]{1,0:T(8,128)(2,1)}, u32[]{:S(2)}) copy-start(bf16[128,4096]{1,0:T(8,128)(2,1)} %get-tuple-element.60.gc_ref) | copy-start | bytes 3145732
  78.5 1.0 copy-start.5
  79.5 1.0 copy-start.6
  92.0 1.0 copy-start.12
  93.0 25.2 %copy-start.11 = (bf16[128,4096]{1,0:T(8,128)(2,1)}, bf16[128,4096]{1,0:T(8,128)(2,1)S(1)}, u32[]{:S(2)}) copy-start(bf16[128,4096]{1,0:T(8,128)(2,1)S(1)} %get-tuple-element.77.near_ref) | copy-start | bytes 3145732
  118.1 19.5 %copy-start.4 = (bf16[128,4096]{1,0:T(8,128)(2,1)S(1)}, bf16[128,4096]{1,0:T(8,128)(2,1)}, u32[]{:S(2)}) copy-start(bf16[128,4096]{1,0:T(8,128)(2,1)} %get-tuple-element.56.gc_ref.refs_5_) | copy-start | bytes 3145732
  157.2 22.0 %collective-permute-start.5 = (bf16[24,8192]{1,0:T(8,128)(2,1)S(1)}, bf16[24,8192]{1,0:T(8,128)(2,1)S(1)}, u32[]{:S(2)}, u32[]{:S(2)}) collective-permute-start(bf16[24,8192]{1,0:T(8,128)(2,1)S(1)} %pad_maximum_fusion.3), channel_id=1, source_target_pairs={{1,0},{2,1},{3,2},{4,3},{5,4},{6,5},{7,6},{8,7},{9,8},{10,9},{11,1... | collective-permute-start | bytes 1179656 | tf_op jit(solution)/shard_map/ppermute | solution.py:21
